TPU v7x, 32 devices: a whole 2x2x4 slice. The times are simulated.
32 devices in a mesh: dp: 8 (over y, x, core), head: 4 (over z).
Axes of the slice: x: 2, y: 2, z: 4, core: 2. Of those that a mesh axis runs over, the one named last changes fastest.
Arguments:
- inputs: bfloat16 [16, 1024, 768], P('dp'), may hold values from -6 to 6
- cotangent: bfloat16 [16, 1024, 768], P('dp'), may hold values from -6 to 6
- lengths: int32 [16], P('dp'), may hold values from 100 to 1024, as said below
- proj_master: float32 [3, 768, 768], P(None, 'dp', 'head'), may hold values from -0.3125 to 0.3125
- proj_first: float32 [3, 768, 768], P(None, 'dp', 'head'), may hold values from -0.00024414062 to 0.00024414062
- proj_second: float32 [3, 768, 768], P(None, 'dp', 'head'), may hold values from 7.48811e-09 to 2.9669868e-08
- out_master: float32 [768, 768], P('head', 'dp')
- out_first: float32 [768, 768], P('head', 'dp'), may hold values from -0.00024414062 to 0.00024414062
- out_second: float32 [768, 768], P('head', 'dp'), may hold values from 7.48811e-09 to 2.9669868e-08
- up_master: float32 [768, 3072], P('dp', 'head')
- up_first: float32 [768, 3072], P('dp', 'head'), may hold values from -0.00024414062 to 0.00024414062
- up_second: float32 [768, 3072], P('dp', 'head'), may hold values from 7.48811e-09 to 2.9669868e-08
- down_master: float32 [3072, 768], P('head', 'dp')
- down_first: float32 [3072, 768], P('head', 'dp'), may hold values from -0.00024414062 to 0.00024414062
- down_second: float32 [3072, 768], P('head', 'dp'), may hold values from 7.48811e-09 to 2.9669868e-08
- norm_master: float32 [4, 768], P(None, 'dp')
- norm_first: float32 [4, 768], P(None, 'dp'), may hold values from -0.0007324219 to 0.0007324219
- norm_second: float32 [4, 768], P(None, 'dp'), may hold values from 6.640399e-08 to 2.6844165e-07
Outputs:
- layer_out: bfloat16 [16, 1024, 768], P('dp', 'head')
- input_grad: bfloat16 [16, 1024, 768], P('dp', 'head')
- grad_norm: float32 [], replicated
- proj_new: float32 [3, 768, 768], P(None, 'dp', 'head')
- proj_first_new: float32 [3, 768, 768], P(None, 'dp', 'head')
- proj_second_new: float32 [3, 768, 768], P(None, 'dp', 'head')
- proj_copy: bfloat16 [3, 768, 768], P(None, 'dp', 'head')
- out_new: float32 [768, 768], P('head', 'dp')
- out_first_new: float32 [768, 768], P('head', 'dp')
- out_second_new: float32 [768, 768], P('head', 'dp')
- out_copy: bfloat16 [768, 768], P('head', 'dp')
- up_new: float32 [768, 3072], P('dp', 'head')
- up_first_new: float32 [768, 3072], P('dp', 'head')
- up_second_new: float32 [768, 3072], P('dp', 'head')
- up_copy: bfloat16 [768, 3072], P('dp', 'head')
- down_new: float32 [3072, 768], P('head', 'dp')
- down_first_new: float32 [3072, 768], P('head', 'dp')
- down_second_new: float32 [3072, 768], P('head', 'dp')
- down_copy: bfloat16 [3072, 768], P('head', 'dp')
- norm_new: float32 [4, 768], P(None, 'dp')
- norm_first_new: float32 [4, 768], P(None, 'dp')
- norm_second_new: float32 [4, 768], P(None, 'dp')
- norm_copy: bfloat16 [4, 768], P(None, 'dp')
Inputs may be any that keep to these rules, and one draw needn't show every extreme that they name: `lengths`: some sequence is 1024 codons long.
All inputs are finite; a program needn't handle non-finite values.
Results may differ from a plain program's by a relative error of at most 0.014.
The roundings to bfloat16 on the way count: a program that leaves them out, or rounds other values in their place, can miss the bound.
Values may be sent and summed in bfloat16 or wider, within the bound.
A program may use at most 128 MiB of HBM per device.

v0:
```python
import jax
import jax.numpy as jnp
from jax import lax
from jax.sharding import PartitionSpec as P

HD = 64
STEP = 5


LN_EPSILON = 1e-05
MASK_FILL = -1e30
ROPE_BASE = 10000.0
CLIP_LIMIT = 1.0
BETA_FIRST = 0.9
BETA_SECOND = 0.95
ADAM_EPSILON = 1e-08
WEIGHT_DECAY = 0.1
RATE_MATRIX = 0.03
RATE_NORM = 0.3
INV_ROOT_TWO = 0.7071067811865476
INV_ROOT_TWO_PI = 0.3989422804014327


def norm_forward(values, gain_row, shift_row):
    center = values - jnp.mean(values, axis=-1, keepdims=True)
    inverse = lax.rsqrt(jnp.mean(center * center, axis=-1, keepdims=True) + LN_EPSILON)
    normed = center * inverse
    return (normed * gain_row + shift_row, normed, inverse)


def norm_backward(grad_rows, normed, inverse, gain_row):
    scaled = grad_rows * gain_row
    inner = jnp.mean(scaled * normed, axis=-1, keepdims=True)
    back_rows = inverse * (scaled - jnp.mean(scaled, axis=-1, keepdims=True) - normed * inner)
    return (back_rows, jnp.sum(grad_rows * normed, axis=0), jnp.sum(grad_rows, axis=0))


def rope_tables(length, head_width):
    places = jnp.arange(length).astype(jnp.float32)
    freq_rates = ROPE_BASE ** (
        -(jnp.arange(head_width // 2).astype(jnp.float32) * 2.0 / head_width)
    )
    angles = places[:, None] * freq_rates[None, :]
    cosine_table = jnp.concatenate([jnp.cos(angles), jnp.cos(angles)], axis=-1)
    sine_table = jnp.concatenate([jnp.sin(angles), jnp.sin(angles)], axis=-1)
    return (cosine_table, sine_table)


def rotate(values, cosine_table, sine_table):
    half_width = values.shape[-1] // 2
    turned = jnp.concatenate([-values[..., half_width:], values[..., :half_width]], axis=-1)
    return values * cosine_table[:, None, :] + turned * sine_table[:, None, :]


def rotate_back(grad_vals, cosine_table, sine_table):
    half_width = grad_vals.shape[-1] // 2
    sined = grad_vals * sine_table[:, None, :]
    swapped = jnp.concatenate([sined[..., half_width:], -sined[..., :half_width]], axis=-1)
    return grad_vals * cosine_table[:, None, :] + swapped


def gelu_slope(upper_rows):
    cumulative = 0.5 * (1.0 + lax.erf(upper_rows * INV_ROOT_TWO))
    return cumulative + upper_rows * jnp.exp(-0.5 * upper_rows * upper_rows) * INV_ROOT_TWO_PI


def attend_forward(operands):
    queries, key_rows, value_rows, valid_keys = operands
    length, heads_here, head_width = queries.shape
    block_rows = min(512, length)
    blocked = queries.reshape(length // block_rows, block_rows, heads_here, head_width)

    def one_block(query_block):
        scores = jnp.einsum(
            "qhd,khd->hqk", query_block, key_rows, preferred_element_type=jnp.float32
        )
        scores = jnp.where(valid_keys[None, None, :], scores, MASK_FILL)
        highest = jnp.max(scores, axis=-1, keepdims=True)
        exponent_vals = jnp.exp(scores - highest)
        totals = jnp.sum(exponent_vals, axis=-1, keepdims=True)
        probs_low = (exponent_vals / totals).astype(jnp.bfloat16)
        attended = jnp.einsum(
            "hqk,khd->qhd", probs_low, value_rows, preferred_element_type=jnp.float32
        )
        return (attended.astype(jnp.bfloat16), (highest + jnp.log(totals))[..., 0])

    attended, log_totals = lax.map(one_block, blocked)
    return (attended.reshape(length, heads_here, head_width), log_totals)


def attend_backward(operands):
    queries, key_rows, value_rows, grad_out, log_totals, valid_keys = operands
    length, heads_here, head_width = queries.shape
    block_rows = min(512, length)
    block_count = length // block_rows
    blocked_queries = queries.reshape(block_count, block_rows, heads_here, head_width)
    blocked_grads = grad_out.reshape(block_count, block_rows, heads_here, head_width)

    def one_block(carry_sums, block_item):
        key_sum, value_sum = carry_sums
        query_block, grad_block, log_block = block_item
        scores = jnp.einsum(
            "qhd,khd->hqk", query_block, key_rows, preferred_element_type=jnp.float32
        )
        scores = jnp.where(valid_keys[None, None, :], scores, MASK_FILL)
        probs = jnp.exp(scores - log_block[..., None])
        probs_low = probs.astype(jnp.bfloat16)
        value_sum = value_sum + jnp.einsum(
            "hqk,qhd->khd", probs_low, grad_block, preferred_element_type=jnp.float32
        )
        grad_probs = jnp.einsum(
            "qhd,khd->hqk", grad_block, value_rows, preferred_element_type=jnp.float32
        )
        inner = jnp.sum(probs * grad_probs, axis=-1, keepdims=True)
        grad_scores = (probs * (grad_probs - inner)).astype(jnp.bfloat16)
        grad_query = jnp.einsum(
            "hqk,khd->qhd", grad_scores, key_rows, preferred_element_type=jnp.float32
        )
        key_sum = key_sum + jnp.einsum(
            "hqk,qhd->khd", grad_scores, query_block, preferred_element_type=jnp.float32
        )
        return ((key_sum, value_sum), grad_query)

    start_sums = (
        jnp.zeros((length, heads_here, head_width), jnp.float32),
        jnp.zeros((length, heads_here, head_width), jnp.float32),
    )
    (key_sum, value_sum), grad_queries = lax.scan(
        one_block, start_sums, (blocked_queries, blocked_grads, log_totals)
    )
    return (grad_queries.reshape(length, heads_here, head_width), key_sum, value_sum)


def adam_update(master, first_old, second_old, gradient, clip_factor, step_rate, decay_rate):
    clipped = gradient * clip_factor
    first_new = BETA_FIRST * first_old + (1.0 - BETA_FIRST) * clipped
    second_new = BETA_SECOND * second_old + (1.0 - BETA_SECOND) * clipped * clipped
    fix_first = 1.0 - BETA_FIRST**STEP
    fix_second = 1.0 - BETA_SECOND**STEP
    normalized = first_new / fix_first / (jnp.sqrt(second_new / fix_second) + ADAM_EPSILON)
    master_new = master - step_rate * (normalized + decay_rate * master)
    return (master_new, first_new, second_new, master_new.astype(jnp.bfloat16))


def per_device(
    inputs,
    cotangent,
    lengths,
    proj_master,
    proj_first,
    proj_second,
    out_master,
    out_first,
    out_second,
    up_master,
    up_first,
    up_second,
    down_master,
    down_first,
    down_second,
    norm_master,
    norm_first,
    norm_second,
):
    seq_count, length, model_width = inputs.shape
    columns = proj_master.shape[2]
    local_heads = columns // HD
    tokens = seq_count * length
    head_parts = lax.axis_size("head")
    quarter = length // head_parts
    offset = lax.axis_index("head") * quarter
    lowered = (
        proj_master.astype(jnp.bfloat16),
        out_master.astype(jnp.bfloat16),
        up_master.astype(jnp.bfloat16),
        down_master.astype(jnp.bfloat16),
        norm_master.astype(jnp.bfloat16),
    )
    proj_w, out_w, up_w, down_w, norm_low = (
        lax.all_gather(lowered[0], "dp", axis=1, tiled=True),
        lax.all_gather(lowered[1], "dp", axis=1, tiled=True),
        lax.all_gather(lowered[2], "dp", axis=0, tiled=True),
        lax.all_gather(lowered[3], "dp", axis=1, tiled=True),
        lax.all_gather(lowered[4], "dp", axis=1, tiled=True),
    )
    norm_w = norm_low.astype(jnp.float32)
    cosine_table, sine_table = rope_tables(length, HD)
    valid_keys = jnp.arange(length)[None, :] < lengths[:, None]
    inputs_f = inputs.astype(jnp.float32)
    rows_in = inputs_f.reshape(tokens, model_width)
    hidden_f, normed_one, inverse_one = norm_forward(rows_in, norm_w[0], norm_w[1])
    hidden_one = hidden_f.astype(jnp.bfloat16)
    raw_proj = jnp.einsum("td,jdc->jtc", hidden_one, proj_w, preferred_element_type=jnp.float32)
    shaped = raw_proj.reshape(3, seq_count, length, local_heads, HD)
    queries = (rotate(shaped[0], cosine_table, sine_table) * HD ** (-0.5)).astype(jnp.bfloat16)
    key_rows = rotate(shaped[1], cosine_table, sine_table).astype(jnp.bfloat16)
    value_rows = shaped[2].astype(jnp.bfloat16)
    attended, log_totals = lax.map(attend_forward, (queries, key_rows, value_rows, valid_keys))
    mixed_heads = attended.reshape(tokens, columns)
    branch = jnp.dot(mixed_heads, out_w, preferred_element_type=jnp.float32)
    middle = rows_in + lax.psum(branch, "head")
    hidden_f2, normed_two, inverse_two = norm_forward(middle, norm_w[2], norm_w[3])
    hidden_two = hidden_f2.astype(jnp.bfloat16)
    upper_rows = jnp.dot(hidden_two, up_w, preferred_element_type=jnp.float32)
    gated_rows = jax.nn.gelu(upper_rows, approximate=False).astype(jnp.bfloat16)
    ffn_part = jnp.dot(gated_rows, down_w, preferred_element_type=jnp.float32)
    summed = (middle + lax.psum(ffn_part.astype(jnp.bfloat16), "head").astype(jnp.float32)).reshape(
        seq_count, length, model_width
    )
    layer_out = lax.dynamic_slice_in_dim(summed, offset, quarter, 1).astype(jnp.bfloat16)
    back_full = cotangent.astype(jnp.float32) * valid_keys[:, :, None].astype(jnp.float32)
    back_rows = back_full.reshape(tokens, model_width)
    back_low = back_rows.astype(jnp.bfloat16)
    grad_down = jnp.einsum("tf,td->fd", gated_rows, back_low, preferred_element_type=jnp.float32)
    grad_gated = jnp.einsum("td,fd->tf", back_low, down_w, preferred_element_type=jnp.float32)
    grad_upper = (grad_gated * gelu_slope(upper_rows)).astype(jnp.bfloat16)
    grad_up = jnp.einsum("td,tf->df", hidden_two, grad_upper, preferred_element_type=jnp.float32)
    grad_two = jnp.einsum("tf,df->td", grad_upper, up_w, preferred_element_type=jnp.float32)
    grad_two = lax.psum(grad_two, "head")
    back_two, gain_two, shift_two = norm_backward(grad_two, normed_two, inverse_two, norm_w[2])
    grad_middle = back_rows + back_two
    grad_branch = grad_middle.astype(jnp.bfloat16)
    grad_out = jnp.einsum("tc,td->cd", mixed_heads, grad_branch, preferred_element_type=jnp.float32)
    grad_mixed = jnp.einsum("td,cd->tc", grad_branch, out_w, preferred_element_type=jnp.float32)
    grad_mixed = grad_mixed.astype(jnp.bfloat16).reshape(seq_count, length, local_heads, HD)
    grad_queries, grad_keys, grad_values = lax.map(
        attend_backward, (queries, key_rows, value_rows, grad_mixed, log_totals, valid_keys)
    )
    grad_raw = jnp.stack(
        [
            rotate_back(grad_queries * HD ** (-0.5), cosine_table, sine_table),
            rotate_back(grad_keys, cosine_table, sine_table),
            grad_values,
        ]
    )
    grad_raw = grad_raw.astype(jnp.bfloat16).reshape(3, tokens, columns)
    grad_proj = jnp.einsum("td,jtc->jdc", hidden_one, grad_raw, preferred_element_type=jnp.float32)
    grad_one = jnp.einsum("jtc,jdc->td", grad_raw, proj_w, preferred_element_type=jnp.float32)
    grad_one = lax.psum(grad_one, "head")
    back_one, gain_one, shift_one = norm_backward(grad_one, normed_one, inverse_one, norm_w[0])
    grad_rows = (grad_middle + back_one).reshape(seq_count, length, model_width)
    input_grad = lax.dynamic_slice_in_dim(grad_rows, offset, quarter, 1).astype(jnp.bfloat16)
    grad_norm_rows = jnp.stack([gain_one, shift_one, gain_two, shift_two])
    reduced = (
        lax.psum_scatter(grad_proj, "dp", scatter_dimension=1, tiled=True),
        lax.psum_scatter(grad_out, "dp", scatter_dimension=1, tiled=True),
        lax.psum_scatter(grad_up, "dp", scatter_dimension=0, tiled=True),
        lax.psum_scatter(grad_down, "dp", scatter_dimension=1, tiled=True),
        lax.psum_scatter(grad_norm_rows, "dp", scatter_dimension=1, tiled=True),
    )
    squares = (
        jnp.sum(reduced[0] * reduced[0])
        + jnp.sum(reduced[1] * reduced[1])
        + jnp.sum(reduced[2] * reduced[2])
    )
    squares = (
        squares + jnp.sum(reduced[3] * reduced[3]) + jnp.sum(reduced[4] * reduced[4]) / head_parts
    )
    total_squares = lax.psum(squares, ("dp", "head"))
    grad_norm = jnp.sqrt(total_squares)
    clip_factor = jnp.minimum(1.0, CLIP_LIMIT / (grad_norm + 1e-06))
    proj_up = adam_update(
        proj_master, proj_first, proj_second, reduced[0], clip_factor, RATE_MATRIX, WEIGHT_DECAY
    )
    out_up = adam_update(
        out_master, out_first, out_second, reduced[1], clip_factor, RATE_MATRIX, WEIGHT_DECAY
    )
    up_up = adam_update(
        up_master, up_first, up_second, reduced[2], clip_factor, RATE_MATRIX, WEIGHT_DECAY
    )
    down_up = adam_update(
        down_master, down_first, down_second, reduced[3], clip_factor, RATE_MATRIX, WEIGHT_DECAY
    )
    norm_up = adam_update(
        norm_master, norm_first, norm_second, reduced[4], clip_factor, RATE_NORM, 0.0
    )
    return (
        layer_out,
        input_grad,
        grad_norm,
        proj_up[0],
        proj_up[1],
        proj_up[2],
        proj_up[3],
        out_up[0],
        out_up[1],
        out_up[2],
        out_up[3],
        up_up[0],
        up_up[1],
        up_up[2],
        up_up[3],
        down_up[0],
        down_up[1],
        down_up[2],
        down_up[3],
        norm_up[0],
        norm_up[1],
        norm_up[2],
        norm_up[3],
    )


def solution(mesh):
    placed = (
        P("dp", None, None),
        P("dp", None, None),
        P("dp"),
        P(None, "dp", "head"),
        P(None, "dp", "head"),
        P(None, "dp", "head"),
        P("head", "dp"),
        P("head", "dp"),
        P("head", "dp"),
        P("dp", "head"),
        P("dp", "head"),
        P("dp", "head"),
        P("head", "dp"),
        P("head", "dp"),
        P("head", "dp"),
        P(None, "dp"),
        P(None, "dp"),
        P(None, "dp"),
    )
    return jax.shard_map(
        per_device,
        mesh=mesh,
        in_specs=placed,
        out_specs=(
            P("dp", "head", None),
            P("dp", "head", None),
            P(),
            P(None, "dp", "head"),
            P(None, "dp", "head"),
            P(None, "dp", "head"),
            P(None, "dp", "head"),
            P("head", "dp"),
            P("head", "dp"),
            P("head", "dp"),
            P("head", "dp"),
            P("dp", "head"),
            P("dp", "head"),
            P("dp", "head"),
            P("dp", "head"),
            P("head", "dp"),
            P("head", "dp"),
            P("head", "dp"),
            P("head", "dp"),
            P(None, "dp"),
            P(None, "dp"),
            P(None, "dp"),
            P(None, "dp"),
        ),
        check_vma=False,
    )
```

profile of v0, /device:TPU:0, one launch (start us, length us, event | category | flops | bytes accessed | tf_op | source)
XLA Modules:
  0.0 1055.4 jit_solution(12091812570609352047)
XLA Ops:
  9.0 10.5 all-gather
  20.1 2.4 convert_reduce_fusion
  22.5 2.9 fusion.49
  25.7 14.3 %all_gather.16 = bf16[3,768,192]{2,0,1:T(4,128)(2,1)} all-gather(bf16[3,96,192]{2,0,1:T(4,128)(2,1)S(1)} %copy.145), channel_id=1, replica_groups=mesh['dp'=8,'head'=4] {'dp'}, dimensions={1}, use_global_device_ids=true | all-gather | bytes 995328 | tf_op jit(solution)/shard_map/all_gather | solution.py:180
  40.0 3.4 copy.146
  50.0 10.3 all_gather.17
  61.7 2.7 convert_element_type.142
  65.5 2.6 squeeze.47
  70.9 2.5 fusion.75
  73.4 39.9 %while.54 = (s32[]{:T(128)}, bf16[2,1024,3,64]{1,0,3,2:T(2,128)(2,1)}, f32[2,2,3,512]{3,2,1,0:T(4,128)}, bf16[2,1024,3,64]{1,3,2,0:T(8,128)(2,1)}, bf16[2,1024,3...) while((s32[]{:T(128)}, ...), condition=%wide.region_7.8_spmd, body=%wide.region_2.7_spmd.sunk | while | flops 416905728 | bytes 32730472 | solution.py:198
  76.1 8.6 while.57
  87.1 5.4 dynamic_update_slice.46
  96.0 8.6 while.57
  107.0 5.4 dynamic_update_slice.46
  115.5 3.7 fusion.109
  123.9 3.3 copy-done.5
  129.1 213.4 %all-reduce.5.cloned.1.call-done = f32[2048,768]{1,0:T(8,128)} async-done(((f32[2048,768]{1,0:T(8,128)}), f32[2048,768]{1,0:T(8,128)}) %all-reduce.5.cloned.1.call-update) | async-done | bytes 6291472 | tf_op jit(solution)/shard_map/psum | solution.py:201
  342.5 3.5 fusion.104
  348.7 2.3 add_convert_fusion
  351.0 18.4 %fusion.41 = (bf16[2048,768]{1,0:T(8,128)(2,1)}, f32[2048,768]{1,0:T(8,128)}) fusion(bf16[2048,768]{1,0:T(8,128)(2,1)} %add_convert_fusion, bf16[768,768]{1,0:T(8,128)(2,1)} %all-gather.4.cloned.1.call-done), kind=kOutput, calls=%fused_computation.62 | convolution fusion | flops 2518155264 | bytes 13762560 | tf_op jit(solution)/shard_map/dot_general | solution.py:204
  369.4 6.4 fusion.47
  377.5 4.5 fusion.110
  382.1 6.5 convolution_convert_fusion
  388.8 6.9 fusion.111
  395.8 5.9 fusion.112
  401.8 202.1 %all-reduce.9.cloned.1.call-done = f32[2048,768]{1,0:T(8,128)} async-done(((f32[2048,768]{1,0:T(8,128)}), f32[2048,768]{1,0:T(8,128)}) %all-reduce.9.cloned.1.call-update) | async-done | bytes 6291472 | tf_op jit(solution)/shard_map/psum | solution.py:219
  604.0 7.5 multiply_reduce_fusion.1
  611.4 6.1 bitcast_add_fusion
  617.6 2.6 copy-done.4
  623.1 61.1 %while.56 = (s32[]{:T(128)}, f32[2,1024,3,64]{1,3,2,0:T(8,128)}, f32[2,1024,3,64]{1,3,2,0:T(8,128)}, bf16[2,1024,3,64]{1,3,2,0:T(8,128)(2,1)}, bf16[2,1024,3,64]...) while((s32[]{:T(128)}, f32[2,1024,3,64]{1,3,2,0:T(8,128)}, ...), condition=%wide.region_19.20_spmd, body=%wide.region_15.19_spmd.sunk | while | flops 1026292224 | bytes 73215464 | solution.py:226
  628.7 18.2 %while.58 = (s32[]{:T(128)}, f32[1024,3,64]{0,2,1:T(8,128)S(1)}, f32[1024,3,64]{0,2,1:T(8,128)S(1)}, f32[2,512,3,64]{1,3,2,0:T(8,128)}, bf16[2,512,3,64]{1,3,2,0...) while((s32[]{:T(128)}, f32[1024,3,64]{0,2,1:T(8,128)S(1)}, ...), condition=%wide.region_18.18_spmd.clone, body=%wide.region_16.17_spmd.clone.sunk | while | flops 1026292224 | bytes 59032788 | solution.py:128
  646.9 2.7 copy.221
  659.0 18.3 %while.58 = (s32[]{:T(128)}, f32[1024,3,64]{0,2,1:T(8,128)S(1)}, f32[1024,3,64]{0,2,1:T(8,128)S(1)}, f32[2,512,3,64]{1,3,2,0:T(8,128)}, bf16[2,512,3,64]{1,3,2,0...) while((s32[]{:T(128)}, f32[1024,3,64]{0,2,1:T(8,128)S(1)}, ...), condition=%wide.region_18.18_spmd.clone, body=%wide.region_16.17_spmd.clone.sunk | while | flops 1026292224 | bytes 59032788 | solution.py:128
  677.3 2.7 copy.221
  692.9 5.1 fusion.84
  700.3 2.8 copy.164
  703.1 3.2 stack.29
  708.5 4.9 fusion.81
  713.4 2.9 copy.174
  716.3 2.8 reshape.234
  719.4 7.1 convolution_bitcast_fusion.2
  730.2 5.6 convert_add_fusion
  742.8 33.3 %reduce-scatter.16.cloned.1.call-done = f32[96,576]{1,0:T(8,128)} async-done(((f32[768,576]{1,0:T(8,128)}), f32[96,576]{1,0:T(8,128)}) %reduce-scatter.16.cloned.1.call-update) | async-done | bytes 221200
  782.4 168.2 %all-reduce.11.cloned.1.call-done = f32[2048,768]{1,0:T(8,128)} async-done(((f32[2048,768]{1,0:T(8,128)}), f32[2048,768]{1,0:T(8,128)}) %all-reduce.11.cloned.1.call-update) | async-done | bytes 6291472 | tf_op jit(solution)/shard_map/psum | solution.py:239
  950.6 4.7 fusion.61
  958.8 6.9 fusion.60
  965.8 25.9 %reduce-scatter.20.cloned.1.call-done = f32[96,4]{1,0:T(8,128)} async-done(((f32[768,4]{1,0:T(8,128)}), f32[96,4]{1,0:T(8,128)}) %reduce-scatter.20.cloned.1.call-update) | async-done | bytes 1552
  995.9 39.3 %psum.39 = f32[]{:T(128)} all-reduce(f32[]{:T(128)S(6)} %add.236), channel_id=1, replica_groups=mesh['dp'=8,'head'=4] {'dp','head'}, use_global_device_ids=true, to_apply=%region_37.38 | all-reduce | flops 1 | bytes 8 | tf_op jit(solution)/shard_map/psum | solution.py:259
  (335 shorter events, 159.2 us)
Async XLA Ops:
  8.0 35.5 %copy-start.1 = (bf16[2,1024,768]{2,1,0:T(8,128)(2,1)S(1)}, bf16[2,1024,768]{2,1,0:T(8,128)(2,1)}, u32[]{:S(2)}) copy-start(bf16[2,1024,768]{2,1,0:T(8,128)(2,1)} %param.26) | copy-start | bytes 9437188
  8.0 17.5 %copy-start.25 = (f32[3,96,192]{2,1,0:T(8,128)S(1)}, f32[3,96,192]{2,1,0:T(8,128)}, u32[]{:S(2)}) copy-start(f32[3,96,192]{2,1,0:T(8,128)} %param.29) | copy-start | bytes 663556
  8.0 334.5 %all-reduce.5.cloned.1.call-start = ((), (), s32[]{:S(2)}) async-start(), calls=%async_computation.5 | async-start | bytes 12582912 | tf_op jit(solution)/shard_map/psum | solution.py:201
  20.1 24.7 %copy-start.44 = (f32[768]{0:T(1024)}, f32[768]{0:T(1024)S(1)}, u32[]{:S(2)}) copy-start(f32[768]{0:T(1024)S(1)} %get-tuple-element.467) | copy-start | bytes 9220
  43.5 3.4 copy-start.38
  43.5 3.4 copy-start.40
  44.8 3.1 copy-start.14
  46.9 3.0 copy-start.32
  73.4 42.1 %copy-start.13 = (bf16[192,768]{0,1:T(8,128)(2,1)S(1)}, bf16[192,768]{0,1:T(8,128)(2,1)}, u32[]{:S(2)}) copy-start(bf16[192,768]{0,1:T(8,128)(2,1)} %all_gather.17) | copy-start | bytes 884740
  76.1 11.0 %copy-start.30 = (bf16[2,1024,3,64]{1,0,3,2:T(2,128)(2,1)S(1)}, bf16[2,1024,3,64]{1,0,3,2:T(2,128)(2,1)}, u32[]{:S(2)}) copy-start(bf16[2,1024,3,64]{1,0,3,2:T(2,128)(2,1)} %get-tuple-element.935) | copy-start | bytes 2359300 | tf_op jit(solution)/shard_map/while
  96.0 11.0 %copy-start.30 = (bf16[2,1024,3,64]{1,0,3,2:T(2,128)(2,1)S(1)}, bf16[2,1024,3,64]{1,0,3,2:T(2,128)(2,1)}, u32[]{:S(2)}) copy-start(bf16[2,1024,3,64]{1,0,3,2:T(2,128)(2,1)} %get-tuple-element.935) | copy-start | bytes 2359300 | tf_op jit(solution)/shard_map/while
  119.2 4.1 copy-start.16
  119.2 4.1 copy-start.46
  119.2 231.7 %all-gather.4.cloned.1.call-start = ((), (), s32[]{:S(2)}) async-start(), calls=%async_computation.6 | async-start | bytes 1327104 | tf_op jit(solution)/shard_map/all_gather | solution.py:182
  121.1 248.2 %all-gather.6.cloned.1.call-start = ((), (), s32[]{:S(2)}) async-start(), calls=%async_computation.7 | async-start | bytes 1327104 | tf_op jit(solution)/shard_map/all_gather | solution.py:183
  123.2 480.7 %all-reduce.9.cloned.1.call-start = ((), (), s32[]{:S(2)}) async-start(), calls=%async_computation.9 | async-start | bytes 12582912 | tf_op jit(solution)/shard_map/psum | solution.py:219
  123.9 3.3 copy-start.5
  127.2 215.4 %copy-start.2 = (bf16[2,1024,768]{2,1,0:T(8,128)(2,1)S(1)}, bf16[2,1024,768]{2,1,0:T(8,128)(2,1)}, u32[]{:S(2)}) copy-start(bf16[2,1024,768]{2,1,0:T(8,128)(2,1)} %param.26) | copy-start | bytes 9437188
  351.0 18.4 %copy-start.17 = (bf16[2048,768]{1,0:T(8,128)(2,1)S(1)}, bf16[2048,768]{1,0:T(8,128)(2,1)}, u32[]{:S(2)}) copy-start(bf16[2048,768]{1,0:T(8,128)(2,1)} %bitcast_convert_fusion) | copy-start | bytes 9437188
  369.4 8.1 copy-start.53
  382.0 348.1 %all-reduce.7.cloned.1.call-start = ((), (), s32[]{:S(2)}) async-start(), calls=%async_computation.8 | async-start | bytes 6291456 | tf_op jit(solution)/shard_map/psum | solution.py:207
  388.6 348.1 %reduce-scatter.12.cloned.1.call-start = ((), (), s32[]{:S(2)}) async-start(), calls=%async_computation.11 | async-start | bytes 2654208 | tf_op jit(solution)/shard_map/reduce_scatter | solution.py:247
  395.7 342.6 %reduce-scatter.14.cloned.1.call-start = ((), (), s32[]{:S(2)}) async-start(), calls=%async_computation.12 | async-start | bytes 2654208 | tf_op jit(solution)/shard_map/reduce_scatter | solution.py:248
  401.8 209.7 %copy-start.43 = (f32[2048]{0:T(1024)S(1)}, f32[2048]{0:T(1024)}, u32[]{:S(2)}) copy-start(f32[2048]{0:T(1024)} %copy-done.42) | copy-start | bytes 24580
  401.8 339.4 %reduce-scatter.18.cloned.1.call-start = ((), (), s32[]{:S(2)}) async-start(), calls=%async_computation.14 | async-start | bytes 884736
  604.0 7.5 copy-start.6
  623.1 61.2 %copy-start.28 = (f32[1024,64]{0,1:T(8,128)S(1)}, f32[1024,64]{0,1:T(8,128)}, u32[]{:S(2)}) copy-start(f32[1024,64]{0,1:T(8,128)} %get-tuple-element.580) | copy-start | bytes 786436
  684.3 3.7 copy-start.11
  686.2 3.0 copy-start.19
  689.1 3.8 copy-start.10
  698.0 10.5 copy-start.15
  698.0 78.1 %reduce-scatter.16.cloned.1.call-start = ((), (), s32[]{:S(2)}) async-start(), calls=%async_computation.13 | async-start | bytes 2211840
  719.2 231.4 %all-reduce.11.cloned.1.call-start = ((), (), s32[]{:S(2)}) async-start(), calls=%async_computation.10 | async-start | bytes 12582912 | tf_op jit(solution)/shard_map/psum | solution.py:239
  726.6 265.1 %reduce-scatter.20.cloned.1.call-start = ((), (), s32[]{:S(2)}) async-start(), calls=%async_computation.15 | async-start | bytes 442368
  730.1 9.9 copy-start.48
  730.1 10.5 copy-start.47
  730.1 220.4 %copy-start.3 = (bf16[2,1024,768]{2,1,0:T(8,128)(2,1)S(1)}, bf16[2,1024,768]{2,1,0:T(8,128)(2,1)}, u32[]{:S(2)}) copy-start(bf16[2,1024,768]{2,1,0:T(8,128)(2,1)} %param.26) | copy-start | bytes 9437188
  730.1 220.4 %copy-start.39 = (f32[2048]{0:T(1024)S(1)}, f32[2048]{0:T(1024)}, u32[]{:S(2)}) copy-start(f32[2048]{0:T(1024)} %copy-done.38) | copy-start | bytes 24580
  730.1 220.4 %copy-start.41 = (f32[2048]{0:T(1024)S(1)}, f32[2048]{0:T(1024)}, u32[]{:S(2)}) copy-start(f32[2048]{0:T(1024)} %copy-done.40) | copy-start | bytes 24580
  950.5 5.9 copy-start.50
  950.6 5.9 copy-start.51
  965.7 78.1 %copy-start.21 = (f32[768,96]{0,1:T(8,128)S(1)}, f32[768,96]{0,1:T(8,128)}, u32[]{:S(2)}) copy-start(f32[768,96]{0,1:T(8,128)} %param.38) | copy-start | bytes 884740
  965.7 78.1 %copy-start.24 = (f32[768,96]{0,1:T(8,128)S(1)}, f32[768,96]{0,1:T(8,128)}, u32[]{:S(2)}) copy-start(f32[768,96]{0,1:T(8,128)} %reduce-scatter.14.cloned.1.call-done) | copy-start | bytes 884740
  965.7 78.1 %copy-start.33 = (f32[768,96]{0,1:T(8,128)S(1)}, f32[768,96]{0,1:T(8,128)}, u32[]{:S(2)}) copy-start(f32[768,96]{0,1:T(8,128)} %param.39) | copy-start | bytes 884740
  965.7 78.1 %copy-start.34 = (f32[768,96]{0,1:T(8,128)S(1)}, f32[768,96]{0,1:T(8,128)}, u32[]{:S(2)}) copy-start(f32[768,96]{0,1:T(8,128)} %param.40) | copy-start | bytes 884740
  965.7 79.2 %copy-start.22 = (f32[96,768]{1,0:T(8,128)S(1)}, f32[96,768]{1,0:T(8,128)}, u32[]{:S(2)}) copy-start(f32[96,768]{1,0:T(8,128)} %param.35) | copy-start | bytes 884740
  965.7 79.2 %copy-start.23 = (f32[96,768]{1,0:T(8,128)S(1)}, f32[96,768]{1,0:T(8,128)}, u32[]{:S(2)}) copy-start(f32[96,768]{1,0:T(8,128)} %reduce-scatter.12.cloned.1.call-done) | copy-start | bytes 884740
  965.7 79.2 %copy-start.35 = (f32[96,768]{1,0:T(8,128)S(1)}, f32[96,768]{1,0:T(8,128)}, u32[]{:S(2)}) copy-start(f32[96,768]{1,0:T(8,128)} %param.36) | copy-start | bytes 884740
  (26 other events, 43.2 us)
Sparse Core Ops, SparseCore 0:
  119.4 223.1 all-reduce.4
  382.1 221.7 all-reduce.8
  606.3 120.0 all-reduce.6
  728.6 221.8 all-reduce.10
Sparse Core Ops, SparseCore 1:
  122.2 24.1 all-gather.3
  148.7 23.9 all-gather.5
  395.8 41.8 reduce-scatter.11
  441.4 42.3 reduce-scatter.13
  698.1 34.3 reduce-scatter.17
  735.9 40.1 reduce-scatter.15
  958.8 32.8 reduce-scatter.19
where the time goes:
time: 1060 us
  waiting for transfers between devices  643 us (61%)
  local copies, waits for them, and re-layouts  119 us (11%)
  matrix products  109 us (10%)
  other arithmetic  85.8 us (8%)
  blocking collectives  74.4 us (7%)
  between operations  21.4 us (2%)
    psum x1, waiting for transfers between devices, per_device(): middle = rows_in + lax.psum(branch, 'head')  213 us
    psum x1, waiting for transfers between devices, per_device(): grad_two = lax.psum(grad_two, 'head')  202 us
    psum x1, waiting for transfers between devices, per_device(): grad_one = lax.psum(grad_one, 'head')  168 us
    unnamed x14, waiting for transfers between devices  59.4 us
    psum x1, blocking collectives, per_device(): total_squares = lax.psum(squares, ('dp', 'head'))  39.3 us
    unnamed x120, local copies, waits for them, and re-layouts  34.3 us
  transfers between devices with their start and end apart: 11, of which 5 were waited for; matrix products, arithmetic and copies ran while one was open for 18% of the time, Pallas kernels for 0%

commit v1 on v0

v1 whole, which is shorter than its diff:
```python
import functools

import jax
import jax.numpy as jnp
import numpy as np
from jax import lax
from jax.experimental import pallas as pl
from jax.experimental.pallas import tpu as pltpu
from jax.sharding import PartitionSpec as P

HD = 64
STEP = 5
LN_EPSILON = 1e-05
MASK_FILL = -1e30
ROPE_BASE = 10000.0
CLIP_LIMIT = 1.0
BETA_FIRST = 0.9
BETA_SECOND = 0.95
ADAM_EPSILON = 1e-08
WEIGHT_DECAY = 0.1
RATE_MATRIX = 0.03
RATE_NORM = 0.3
INV_ROOT_TWO = 0.7071067811865476
INV_ROOT_TWO_PI = 0.3989422804014327

F32 = jnp.float32
BF16 = jnp.bfloat16
MESH = pl.DeviceIdType.MESH
SUB = 256
PIECES = 9


def dot(a, b):
    return lax.dot_general(a, b, (((1,), (0,)), ((), ())), preferred_element_type=F32)


def dot_t(a, b):
    return lax.dot_general(a, b, (((1,), (1,)), ((), ())), preferred_element_type=F32)


def row_mean(v):
    return jnp.mean(v, axis=-1, keepdims=True)


def normalize(v):
    center = v - row_mean(v)
    inverse = lax.rsqrt(row_mean(center * center) + LN_EPSILON)
    return center * inverse, inverse


def lanes(rows):
    return lax.broadcasted_iota(jnp.int32, (rows, 128), 1)


def head_lanes(lane, half):
    return lane < HD if half == 0 else lane >= HD


def three_parts(col):
    hi = col.astype(BF16).astype(F32)
    mid = (col - hi).astype(BF16).astype(F32)
    return hi, mid, col - hi - mid


def spare_columns(lane, base, values, other):
    out = other
    for i, v in reversed(list(enumerate(values))):
        out = jnp.where(lane == base + i, v, out)
    return out


def rope(v, cos, sin_a, sin_b):
    return v * cos + pltpu.roll(v, 96, 1) * sin_a + pltpu.roll(v, 32, 1) * sin_b


def rope_back(v, cos, sin_a, sin_b):
    return v * cos - pltpu.roll(v, 96, 1) * sin_a - pltpu.roll(v, 32, 1) * sin_b


def layer_kernel(inner, T, D, R, *refs):
    (
        x_in, ct_in, lens_in, pack, norm_in, cos_ref, sina_ref, sinb_ref,
        lo_out, ig_out, g_out, gn_out, sq_out,
        W, GA, xs, cc, cT, h1, h1T, h2, h2T, x1, qe, ke, ve, doe, kT,
        opair, osib, o256, wsib, zb, du, dh2, dh2r, dqT, fsend, frecv, dsend, drecv, stage,
        lens_v, nw, nl, gl1, gl2, sl1, sl2, LX, LY, ZL,
        in_s, in_r, o_s, o_r, ws_s, ws_r, d2_s, d2_r, f_s, f_r, d1_s, d1_r, out_s, out_r, n_s, n_r, e_s, e_r,
        s1s, s1r, a2s, a2r, r1s, r1r, r2s, r2r, zss, zsr, loc,
    ) = refs
    RC = 2 * R
    TB = 256
    NB = T // TB
    HALF = T // 2
    d = lax.axis_index("dp")
    z = lax.axis_index("head")
    core = d % 2
    k = d // 2
    own = z // 2
    li = z % 2
    sib = (d + 1 - 2 * core, z)
    n_dp = lax.axis_size("dp")

    def rc(src, dst, ss, rs, dev):
        return pltpu.make_async_remote_copy(
            src_ref=src, dst_ref=dst, send_sem=ss, recv_sem=rs, device_id=dev, device_id_type=MESH
        )

    column = []
    for da in range(2):
        for dz in range(4):
            if da + dz > 0:
                dd = d if da == 0 else sib[0]
                column.append((da * 4 + dz, (dd, (z + dz) % 4)))
    if inner:
        kx = k + 1 - 2 * (k % 2)
        ky = (k + 2) % 4
        kd = 3 - k
        xdev = (2 * kx + core, z)
        ydev = (2 * ky + core, z)
        ddev = (2 * kd + core, z)
        plane = [xdev, ydev, ddev]
    else:
        plane = []
    everyone = [dev for _, dev in column] + plane
    barrier = pltpu.get_barrier_semaphore()
    for dev in everyone:
        pl.semaphore_signal(barrier, inc=1, device_id=dev, device_id_type=MESH)
    pl.semaphore_wait(barrier, len(everyone))

    def in_remote(i):
        src = (x_in.at[li], ct_in.at[li], lens_in)[i]
        dst = (xs, cc, lens_v)[i]
        return rc(src, dst, in_s.at[i], in_r.at[i], sib)

    def in_local(i):
        src = (x_in.at[li], ct_in.at[li], lens_in)[i]
        dst = (xs, cc, lens_v)[i]
        return pltpu.make_async_copy(src, dst, loc.at[i])

    @pl.when(core == own)
    def _():
        for i in (2, 0, 1):
            in_remote(i).start()
            in_local(i).start()

    def piece(s):
        if isinstance(s, int):
            if s < 3:
                return 0, SUB * s
            return 1 + (s - 3) % 2, SUB * ((s - 3) // 2)
        return 1 + (s - 3) % 2, pl.multiple_of(((s - 3) // 2) * SUB, SUB)

    def rows_at(block, size):
        return pl.ds(pl.multiple_of(block * size, 16), size)

    def cols_at(e, col):
        if isinstance(e, int) and isinstance(col, int):
            return pl.ds(e * 768 + col, SUB)
        return pl.ds(pl.multiple_of(e * 768 + col, 128), SUB)

    def ag1(s, dz, a, e, dev):
        j, col = piece(s)
        src = pack.at[j, :, pl.ds(col, SUB)]
        dst = W.at[j, rows_at(2 * k + a, R), cols_at(e, col)]
        return rc(src, dst, s1s.at[s, dz], s1r.at[s, a * 2 + e], dev)

    def ag1_start(s):
        j, col = piece(s)
        for dz in range(1, 4):
            ag1(s, dz, core, li, (2 * k + own, (z + dz) % 4)).start()

        @pl.when(core == own)
        def _():
            pltpu.make_async_copy(
                pack.at[j, :, pl.ds(col, SUB)], W.at[j, rows_at(d, R), cols_at(li, col)], s1r.at[s, core * 2 + li]
            ).start()

        @pl.when(core != own)
        def _():
            ag1(s, 0, core, li, sib).start()

    def ag2(s, e, to, rows, dev, slot):
        j, col = piece(s)
        region = W.at[j, rows_at(rows, RC), cols_at(e, col)]
        return rc(region, region, a2s.at[s, e, to], a2r.at[s, e, slot], dev)

    def ag2_start(s):
        for a in range(2):
            for e in range(2):
                ag1(s, 1, a, e, sib).wait_recv()
        for e in range(2):
            ag2(s, e, 0, k, xdev, 0).start()
            ag2(s, e, 1, k, ydev, 1).start()

    def ag3_start(s):
        ag2(s, 0, 2, kx, ydev, 0).wait_recv()
        ag2(s, 0, 2, kx, ydev, 2).start()
        ag2(s, 1, 2, ky, xdev, 1).wait_recv()
        ag2(s, 1, 2, ky, xdev, 2).start()

    def ag_wait(s):
        ag2(s, 0, 1, ky, ydev, 1).wait_recv()
        ag2(s, 0, 2, kd, ydev, 2).wait_recv()
        ag2(s, 1, 0, kx, xdev, 0).wait_recv()
        ag2(s, 1, 2, kd, xdev, 2).wait_recv()

    def ag_drain(s):
        for dz in range(1, 4):
            ag1(s, dz, core, li, sib).wait_send()

        @pl.when(core != own)
        def _():
            ag1(s, 0, core, li, sib).wait_send()

        for e in range(2):
            for to in range(3):
                ag2(s, e, to, k, xdev, to).wait_send()

    if inner:
        for s in range(PIECES):
            ag1_start(s)
        nl[pl.ds(d, 1)] = norm_in[...].reshape(1, 8, 128)
        rc(nl.at[pl.ds(d, 1)], nl.at[pl.ds(d, 1)], n_s.at[0], n_r.at[0], sib).start()
        rc(nl.at[pl.ds(d, 1)], nl.at[pl.ds(sib[0], 1)], n_s.at[0], n_r.at[0], sib).wait()
        for i, dev in enumerate(plane):
            rc(nl.at[pl.ds(2 * k, 2)], nl.at[pl.ds(2 * k, 2)], n_s.at[1 + i], n_r.at[1 + i], dev).start()
    else:
        w_copy = pltpu.make_async_copy(pack, W, loc.at[3])
        w_copy.start()

    @pl.when(core == own)
    def _():
        for i in range(3):
            in_local(i).wait()

    @pl.when(core != own)
    def _():
        for i in range(3):
            in_remote(i).wait_recv()

    if inner:
        for i, kk in enumerate((kx, ky, kd)):
            rc(nl.at[pl.ds(2 * kk, 2)], nl.at[pl.ds(2 * kk, 2)], n_s.at[1 + i], n_r.at[1 + i], plane[i]).wait()
        nw[...] = jnp.zeros_like(nw)

        def place(i, carry):
            r_i = lax.broadcasted_iota(jnp.int32, (128, D), 0)
            c_i = lax.broadcasted_iota(jnp.int32, (128, D), 1)
            sel = jnp.where((r_i < R) & (c_i == r_i + i * R), 1.0, 0.0).astype(BF16)
            nw[...] += dot(nl[i].astype(BF16), sel)
            return carry

        lax.fori_loop(0, 8, place, 0)
    else:
        nw[...] = norm_in[...]

    length = lens_v[0:1, 0:1]

    def row_valid(start, rows):
        ids = (lax.broadcasted_iota(jnp.int32, (rows, 1), 0) + start).astype(F32)
        return ids < length

    def at(i, size=TB):
        return pl.ds(pl.multiple_of(i * size, size), size)

    def norm_one(i, carry):
        rows = at(i)
        n, _ = normalize(xs[rows, :].astype(F32))
        h = (n * nw[0:1, :] + nw[1:2, :]).astype(BF16)
        h1[rows, :] = h
        h1T[:, rows] = h.T
        c = jnp.where(row_valid(i * TB, TB), cc[rows, :].astype(F32), 0.0).astype(BF16)
        cc[rows, :] = c
        cT[:, rows] = c.T
        return carry

    lax.fori_loop(0, NB, norm_one, 0)

    if inner:
        ag2_start(0)
        ag2_start(1)
        ag3_start(0)
        ag2_start(2)
        ag3_start(1)
        ag_wait(0)
        ag3_start(2)
        ag_wait(1)
    else:
        w_copy.wait()

    lane = lanes(TB)
    low = lane < HD

    def make_pair(p):
        def block(i, carry):
            rows = at(i)
            h = h1[rows, :]
            cos, sa, sb = cos_ref[rows, :], sina_ref[rows, :], sinb_ref[rows, :]
            if p < 2:
                raw = dot(h, W[0, :, p * 768 : p * 768 + 384])
                q, kk, v = raw[:, :128], raw[:, 128:256], raw[:, 256:]
                q = rope(q, cos, sa, sb)
                kk = rope(kk, cos, sa, sb)
            else:
                r0 = dot(h, W[0, :, 384:640])
                r1 = dot(h, W[0, :, 768 + 384 : 768 + 640])
                ra = rope(r0[:, :128], cos, sa, sb)
                rb = rope(r1[:, :128], cos, sa, sb)
                q = jnp.where(low, ra, pltpu.roll(rb, 64, 1))
                kk = jnp.where(low, pltpu.roll(ra, 64, 1), rb)
                v = jnp.where(low, r0[:, 128:], pltpu.roll(r1[:, 128:], 64, 1))
            q = q * HD**-0.5
            bias = jnp.where(row_valid(i * TB, TB), 0.0, MASK_FILL)
            kT[p, :, rows] = kk.astype(BF16).T
            for half in range(2):
                mine = head_lanes(lane, half)
                base = HD - HD * half
                hh = 2 * p + half
                qe[hh, rows, :] = jnp.where(mine, q, jnp.where(lane == base, 1.0, 0.0)).astype(BF16)
                ke[hh, rows, :] = jnp.where(mine, kk, jnp.where(lane == base, bias, 1.0)).astype(BF16)
                ve[hh, rows, :] = jnp.where(mine, v, 1.0).astype(BF16)
            return carry

        lax.fori_loop(0, NB, block, 0)

    def attend(p, i):
        rows = at(i)
        outs = []
        for half in range(2):
            hh = 2 * p + half
            mine = head_lanes(lane, half)
            base = HD - HD * half
            q = qe[hh, rows, :]
            s = dot_t(q, ke[hh])
            top = jnp.max(s, axis=-1, keepdims=True)
            ex = jnp.exp(s - top).astype(BF16)
            o = dot(ex, ve[hh])
            total = o[:, base : base + 1]
            outs.append(o * (1.0 / total))
            hi, mid, lo = three_parts(top + jnp.log(total))
            extra = spare_columns(lane, base, (1.0, -hi, -mid, -lo), 0.0)
            qe[hh, rows, :] = jnp.where(mine, q.astype(F32), extra).astype(BF16)
        opair[p, rows, :] = jnp.where(low, outs[0], outs[1]).astype(BF16)

    def o_copy(p):
        return rc(opair.at[p], osib.at[p], o_s.at[p], o_r.at[p], sib)

    def ws_copy(e):
        return rc(W.at[0, :, pl.ds(e * 768 + 512, 256)], wsib.at[e], ws_s.at[e], ws_r.at[e], sib)

    for p in range(3):
        if inner and p == 2:
            ag_wait(2)
        make_pair(p)

        def attend_two(i, carry, p=p):
            s = 3 + 2 * p + i
            if inner:
                ag2_start(s)
            attend(p, 2 * i)
            if inner:
                ag3_start(s)
            attend(p, 2 * i + 1)
            return carry

        lax.fori_loop(0, NB // 2, attend_two, 0)
        o_copy(p).start()
        if p == 2:
            for e in range(2):
                ws_copy(e).start()

    def wide_o(pairs, e, rows):
        single = pairs[2, rows, :].astype(F32)
        if e == 0:
            single = pltpu.roll(single, 64, 1)
        single = jnp.where(low, 0.0, single).astype(BF16)
        return jnp.concatenate([single, pairs[e, rows, :]], axis=1)

    for p in range(3):
        o_copy(p).wait()
    for e in range(2):
        ws_copy(e).wait()

    def project_out(i, carry):
        rows = at(i)
        acc = xs[rows, :].astype(F32)
        for e in range(2):
            mine = wide_o(opair, e, rows)
            o256[e, rows, :] = mine
            acc = acc + dot_t(mine, W[0, :, e * 768 + 512 : e * 768 + 768])
            acc = acc + dot_t(wide_o(osib, e, rows), wsib[e])
        x1[rows, :] = acc
        n, _ = normalize(acc)
        h = (n * nw[2:3, :] + nw[3:4, :]).astype(BF16)
        h2[rows, :] = h
        h2T[:, rows] = h.T
        return carry

    lax.fori_loop(0, NB, project_out, 0)

    for i3 in range(3):
        if inner:
            ag_wait(3 + 2 * i3)
            ag_wait(4 + 2 * i3)

        def hidden(i, carry, i3=i3):
            rows = at(i % NB)
            cols = cols_at(i // NB, SUB * i3)
            u = dot(h2[rows, :], W[1, :, cols])
            dz = dot(cc[rows, :], W[2, :, cols])
            cumulative = 0.5 * (1.0 + lax.erf(u * INV_ROOT_TWO))
            slope = cumulative + u * jnp.exp(-0.5 * u * u) * INV_ROOT_TWO_PI
            zb[rows, cols] = (u * cumulative).astype(BF16)
            du[rows, cols] = (dz * slope).astype(BF16)
            return carry

        lax.fori_loop(0, 2 * NB, hidden, 0)

    def d2_copy(i):
        return rc(h1.at[at(i), :], dh2r.at[at(i), :], d2_s.at[i], d2_r.at[i], sib)

    def back_two(i, carry):
        rows = at(i)
        v = dot_t(du[rows, :], W[1])
        dh2[rows, :] = v
        h1[rows, :] = v.astype(BF16)
        d2_copy(i).start()
        return carry

    lax.fori_loop(0, NB, back_two, 0)

    other = 1 - core

    def half_rows(which, i):
        return pl.ds(pl.multiple_of(which * HALF + i * TB, TB), TB)

    def f_copy():
        return rc(fsend, frecv, f_s.at[0], f_r.at[0], sib)

    def ffn_other(i, carry):
        fsend[at(i), :] = dot_t(zb[half_rows(other, i), :], W[2]).astype(BF16)
        return carry

    lax.fori_loop(0, NB // 2, ffn_other, 0)
    f_copy().start()

    def grad(s):
        return GA if isinstance(s, int) and s < 3 else W.at[piece(s)[0]]

    def rs1(s, e, b, rows, dev):
        src = grad(s).at[rows_at(rows, RC), cols_at(e, piece(s)[1])]
        return rc(src, LX.at[s, e, b], r1s.at[s, e, b], r1r.at[s, e, b], dev)

    def rs1_start(s):
        rs1(s, 0, 1, kd, xdev).start()
        rs1(s, 1, 1, kd, ydev).start()
        rs1(s, 0, 0, kx, xdev).start()
        rs1(s, 1, 0, ky, ydev).start()

    def rs2(s, e, dev):
        return rc(LX.at[s, e, 1], LY.at[s, e], r2s.at[s, e], r2r.at[s, e], dev)

    def rs2_start(s):
        for e, near, far, dev in ((0, kx, ky, ydev), (1, ky, kx, xdev)):
            rs1(s, e, 1, far, dev).wait_recv()
            mine = grad(s)[rows_at(far, RC), cols_at(e, piece(s)[1])].astype(F32)
            LX[s, e, 1] = (LX[s, e, 1].astype(F32) + mine).astype(BF16)
            rs2(s, e, dev).start()

    def rs3(s, e, a, dev):
        return rc(LX.at[s, e, 0, pl.ds(a * R, R)], ZL.at[s, z], zss.at[s, e * 2 + a], zsr.at[s, z], dev)

    def rs3_start(s):
        for e in range(2):
            rs1(s, e, 0, k, xdev).wait_recv()
            rs2(s, e, ydev).wait_recv()
            mine = grad(s)[rows_at(k, RC), cols_at(e, piece(s)[1])].astype(F32)
            LX[s, e, 0] = (LX[s, e, 0].astype(F32) + LY[s, e].astype(F32) + mine).astype(BF16)
            zt = 2 * core + e
            for a in range(2):
                here = (core == a) & (zt == z)

                @pl.when(here)
                def _(a=a, e=e):
                    pltpu.make_async_copy(LX.at[s, e, 0, pl.ds(a * R, R)], ZL.at[s, z], zsr.at[s, z]).start()

                @pl.when(jnp.logical_not(here))
                def _(a=a, e=e, zt=zt):
                    rs3(s, e, a, (2 * k + a, zt)).start()

    def rs4(s):
        j, col = piece(s)
        total = jnp.zeros((R, SUB), F32)
        for zz in range(4):
            rc(LX.at[s, 0, 0, pl.ds(0, R)], ZL.at[s, zz], zss.at[s, 0], zsr.at[s, zz], sib).wait_recv()
            total = total + ZL[s, zz].astype(F32)
        g_out[j, :, pl.ds(col, SUB)] = total
        return total

    def rs_drain(s):
        for e in range(2):
            for b in range(2):
                rs1(s, e, b, k, xdev).wait_send()
            rs2(s, e, ydev).wait_send()
            zt = 2 * core + e
            for a in range(2):

                @pl.when(jnp.logical_not((core == a) & (zt == z)))
                def _(a=a, e=e):
                    rs3(s, e, a, sib).wait_send()

    def out_copy(ref, which, qi, slot):
        src = stage.at[which, pl.ds(qi * (T // 4), T // 4), :]
        return rc(src, ref.at[li], out_s.at[which, qi], out_r.at[which, slot], (2 * k + own, 2 * core + qi))

    def out_start(ref, which):
        for qi in range(2):
            here = (core == own) & (li == qi)

            @pl.when(here)
            def _(qi=qi):
                src = stage.at[which, pl.ds(qi * (T // 4), T // 4), :]
                pltpu.make_async_copy(src, ref.at[li], out_r.at[which, li]).start()

            @pl.when(jnp.logical_not(here))
            def _(qi=qi):
                out_copy(ref, which, qi, li).start()

    def out_wait(ref, which):
        for slot in range(2):
            src = stage.at[which, pl.ds(0, T // 4), :]
            rc(src, ref.at[slot], out_s.at[which, 0], out_r.at[which, slot], sib).wait_recv()
        for qi in range(2):

            @pl.when(jnp.logical_not((core == own) & (li == qi)))
            def _(qi=qi):
                out_copy(ref, which, qi, 0).wait_send()

    if inner:

        def drain(s, carry):
            ag_drain(s)
            return carry

        for s in range(3):
            ag_drain(s)
        lax.fori_loop(3, PIECES, drain, 0)

    def grad_up(i, carry):
        for e in range(2):
            cols = cols_at(e, pl.multiple_of(i * SUB, SUB))
            W[1, :, cols] = dot(h2T[...], du[:, cols]).astype(BF16)
        if inner:
            rs1_start(3 + 2 * i)
        return carry

    lax.fori_loop(0, 3, grad_up, 0)

    f_copy().wait()

    def ffn_final(i, carry):
        rows = half_rows(core, i)
        y = x1[rows, :] + dot_t(zb[rows, :], W[2]) + frecv[at(i), :].astype(F32)
        stage[0, at(i), :] = y.astype(BF16)
        return carry

    lax.fori_loop(0, NB // 2, ffn_final, 0)
    out_start(lo_out, 0)

    def grad_down(i, carry):
        for e in range(2):
            cols = cols_at(e, pl.multiple_of(i * SUB, SUB))
            W[2, :, cols] = dot(cT[...], zb[:, cols]).astype(BF16)
        if inner:
            rs1_start(4 + 2 * i)
        return carry

    lax.fori_loop(0, 3, grad_down, 0)

    gn_out[...] = jnp.zeros_like(gn_out)

    def norm_back_two(i, carry):
        rows = at(i)
        d2_copy(i).wait()
        e2 = dh2[rows, :] + dh2r[rows, :].astype(F32)
        n, r = normalize(x1[rows, :])
        m = e2 * nw[2:3, :]
        dx = cc[rows, :].astype(F32) + r * (m - row_mean(m) - n * row_mean(m * n))
        dh2[rows, :] = dx
        low_dx = dx.astype(BF16)
        h2[rows, :] = low_dx
        h2T[:, rows] = low_dx.T
        count = jnp.where(i // (NB // 2) == core, 1.0, 0.0)
        gn_out[2:3, :] += count * jnp.sum(e2 * n, axis=0, keepdims=True)
        gn_out[3:4, :] += count * jnp.sum(e2, axis=0, keepdims=True)
        return carry

    lax.fori_loop(0, NB, norm_back_two, 0)
    da, daT = h2, h2T

    def do_block(i, carry):
        rows = at(i)
        parts = [dot(da[rows, :], W[0, :, e * 768 + 512 : e * 768 + 768]) for e in range(2)]
        pairs = [parts[0][:, 128:], parts[1][:, 128:], jnp.where(low, pltpu.roll(parts[0][:, :128], 64, 1), parts[1][:, :128])]
        for p in range(3):
            g = pairs[p].astype(BF16).astype(F32)
            prod = g * opair[p, rows, :].astype(F32)
            for half in range(2):
                mine = head_lanes(lane, half)
                base = HD - HD * half
                delta = jnp.sum(jnp.where(mine, prod, 0.0), axis=-1, keepdims=True)
                hi, mid, lo = three_parts(delta)
                extra = spare_columns(lane, base + 1, (-hi, -mid, -lo), 0.0)
                doe[2 * p + half, rows, :] = jnp.where(mine, g, extra).astype(BF16)
        return carry

    lax.fori_loop(0, NB, do_block, 0)

    def back_keys(p, i):
        rows = at(i)
        cos, sa, sb = cos_ref[rows, :], sina_ref[rows, :], sinb_ref[rows, :]
        dks, dvs = [], []
        for half in range(2):
            hh = 2 * p + half
            sT = dot_t(ke[hh, rows, :], qe[hh])
            pT = jnp.exp(sT)
            dpT = dot_t(ve[hh, rows, :], doe[hh])
            dsT = (pT * dpT).astype(BF16)
            dvs.append(dot(pT.astype(BF16), doe[hh]))
            dks.append(dot(dsT, qe[hh]))
            part = dot(kT[p, half * HD : half * HD + HD, rows], dsT)
            dqT[half * HD : half * HD + HD, :] += part
        dk = rope_back(jnp.where(low, dks[0], dks[1]), cos, sa, sb)
        dv = jnp.where(low, dvs[0], dvs[1])
        put_draw(p, rows, None, dk, dv)

    def put_draw(p, rows, dq, dk, dv):
        if p < 2:
            for i, v in enumerate((dq, dk, dv)):
                if v is not None:
                    du[rows, p * 768 + 128 * i : p * 768 + 128 * i + 128] = v.astype(BF16)
            return
        if dk is not None:
            du[rows, 640:768] = dk.astype(BF16)
            du[rows, 512:640] = jnp.where(low, dv, 0.0).astype(BF16)
            du[rows, 768 + 512 : 768 + 640] = jnp.where(low, pltpu.roll(dv, 64, 1), 0.0).astype(BF16)
        if dq is not None:
            dk = du[rows, 640:768].astype(F32)
            du[rows, 384:512] = jnp.where(low, dq, pltpu.roll(dk, 64, 1)).astype(BF16)
            du[rows, 768 + 384 : 768 + 512] = jnp.where(low, pltpu.roll(dq, 64, 1), dk).astype(BF16)

    def put_queries(p):
        def block(i, carry):
            rows = at(i)
            cos, sa, sb = cos_ref[rows, :], sina_ref[rows, :], sinb_ref[rows, :]
            dq = dqT[:, rows].T * HD**-0.5
            put_draw(p, rows, rope_back(dq, cos, sa, sb), None, None)
            return carry

        lax.fori_loop(0, NB, block, 0)

    for step, p in enumerate((2, 0, 1)):
        dqT[...] = jnp.zeros_like(dqT)

        def back_step(i, carry, p=p, step=step):
            back_keys(p, 2 * i)
            if inner:
                rs2_start(3 + 2 * step + i)
            back_keys(p, 2 * i + 1)
            if inner:
                rs3_start(3 + 2 * step + i)
            return carry

        lax.fori_loop(0, NB // 2, back_step, 0)
        put_queries(p)
        if p == 2:
            for e in range(2):
                b = e * 768
                GA[:, b + 384 : b + 512] = dot(h1T[...], du[:, b + 384 : b + 512]).astype(BF16)
                wide = dot(daT[...], o256[e])
                GA[:, b + 640 : b + 768] = wide[:, 128:].astype(BF16)
                GA[:, b + 512 : b + 640] = (wide[:, :128] + dot(h1T[...], du[:, b + 512 : b + 640])).astype(BF16)
            if inner:
                rs1_start(2)
        else:
            b = p * 768
            GA[:, b : b + 384] = dot(h1T[...], du[:, b : b + 384]).astype(BF16)
            if inner and p == 0:
                rs2_start(2)
    if inner:
        rs1_start(0)
        rs1_start(1)
        rs3_start(2)

    def back_one(rows):
        return dot_t(du[rows, 0:640], W[0, :, 0:640]) + dot_t(du[rows, 768 : 768 + 640], W[0, :, 768 : 768 + 640])

    def d1_copy():
        return rc(dsend, drecv, d1_s.at[0], d1_r.at[0], sib)

    def one_other(i, carry):
        dsend[at(i), :] = back_one(half_rows(other, i)).astype(BF16)
        return carry

    lax.fori_loop(0, NB // 2, one_other, 0)
    d1_copy().start()

    def one_mine(i, carry):
        rows = half_rows(core, i)
        x1[rows, :] = back_one(rows)
        return carry

    lax.fori_loop(0, NB // 2, one_mine, 0)
    if inner:
        rs2_start(0)
        rs2_start(1)
    d1_copy().wait()

    def norm_back_one(i, carry):
        rows = half_rows(core, i)
        e1 = x1[rows, :] + drecv[at(i), :].astype(F32)
        n, r = normalize(xs[rows, :].astype(F32))
        m = e1 * nw[0:1, :]
        dx = dh2[rows, :] + r * (m - row_mean(m) - n * row_mean(m * n))
        stage[1, at(i), :] = dx.astype(BF16)
        gn_out[0:1, :] += jnp.sum(e1 * n, axis=0, keepdims=True)
        gn_out[1:2, :] += jnp.sum(e1, axis=0, keepdims=True)
        return carry

    lax.fori_loop(0, NB // 2, norm_back_one, 0)
    out_start(ig_out, 1)

    def sum_everywhere(ref, l1, l2, which):
        l1[0] = ref[...]
        for slot, dev in column:
            rc(l1.at[0], l1.at[slot], e_s.at[which, slot], e_r.at[which, slot], dev).start()
        total = l1[0]
        for slot, dev in column:
            rc(l1.at[0], l1.at[slot], e_s.at[which, slot], e_r.at[which, slot], dev).wait()
            total = total + l1[slot]
        l2[0] = total
        for i, dev in enumerate(plane):
            rc(l2.at[0], l2.at[1 + i], e_s.at[which, 8 + i], e_r.at[which, 8 + i], dev).start()
        for i, dev in enumerate(plane):
            rc(l2.at[0], l2.at[1 + i], e_s.at[which, 8 + i], e_r.at[which, 8 + i], dev).wait()
            total = total + l2[1 + i]
        ref[...] = total

    if inner:
        rs3_start(0)
        rs3_start(1)
        sum_everywhere(gn_out, gl1, gl2, 0)
        squares = jnp.zeros((R, SUB), F32)

        def last(s, acc):
            g = rs4(s)
            return acc + g * g

        squares = lax.fori_loop(3, PIECES, last, squares)
        for s in (2, 0, 1):
            squares = last(s, squares)
        total = jnp.sum(squares, axis=0, keepdims=True)
        total = total[:, :128] + total[:, 128:]
        sq_out[...] = jnp.where(lax.broadcasted_iota(jnp.int32, (8, 128), 0) == 0, total, 0.0)
        sum_everywhere(sq_out, sl1, sl2, 1)

        def drain_rs(s, carry):
            rs_drain(s)
            return carry

        for s in range(3):
            rs_drain(s)
        lax.fori_loop(3, PIECES, drain_rs, 0)
    else:
        sq_out[...] = jnp.zeros_like(sq_out)
        for j in range(3):
            g_copy = pltpu.make_async_copy(GA if j == 0 else W.at[j], g_out.at[j], loc.at[3 + j])
            g_copy.start()
            g_copy.wait()
    out_wait(lo_out, 0)
    out_wait(ig_out, 1)

    @pl.when(core == own)
    def _():
        for i in range(3):
            in_remote(i).wait_send()


def rope_tables(length):
    places = np.arange(length, dtype=np.float32)
    rates = (ROPE_BASE ** (-(np.arange(HD // 2, dtype=np.float32) * 2.0 / HD))).astype(np.float32)
    angles = places[:, None] * rates[None, :]
    cos = np.tile(np.cos(angles), (1, 4)).astype(np.float32)
    sin = np.tile(np.sin(angles), (1, 4)).astype(np.float32)
    first = (np.arange(128) % HD < HD // 2)[None, :]
    return cos, np.where(first, -sin, 0.0).astype(np.float32), np.where(first, 0.0, sin).astype(np.float32)


def adam_update(master, first_old, second_old, gradient, clip_factor, step_rate, decay_rate):
    clipped = gradient * clip_factor
    first_new = BETA_FIRST * first_old + (1.0 - BETA_FIRST) * clipped
    second_new = BETA_SECOND * second_old + (1.0 - BETA_SECOND) * clipped * clipped
    fix_first = 1.0 - BETA_FIRST**STEP
    fix_second = 1.0 - BETA_SECOND**STEP
    normalized = first_new / fix_first / (jnp.sqrt(second_new / fix_second) + ADAM_EPSILON)
    master_new = master - step_rate * (normalized + decay_rate * master)
    return (master_new, first_new, second_new, master_new.astype(BF16))


def per_device(
    inputs,
    cotangent,
    lengths,
    proj_master,
    proj_first,
    proj_second,
    out_master,
    out_first,
    out_second,
    up_master,
    up_first,
    up_second,
    down_master,
    down_first,
    down_second,
    norm_master,
    norm_first,
    norm_second,
):
    _, T, D = inputs.shape
    R = proj_master.shape[1]
    n_dp = lax.axis_size("dp")
    inner = n_dp == 8
    d = lax.axis_index("dp")
    z = lax.axis_index("head")
    core, own, li = d % 2, z // 2, z % 2
    out_t = out_master.T
    attn = jnp.concatenate(
        [proj_master[0, :, :128], proj_master[1, :, :128], proj_master[2, :, :128]]
        + [proj_master[0, :, 128:], proj_master[1, :, 128:], proj_master[2, :, 128:]]
        + [out_t[:, 128:], out_t[:, :128]],
        axis=1,
    )
    pack = jnp.stack([attn, up_master, down_master.T]).astype(BF16)
    norm_low = norm_master.astype(BF16).astype(F32)
    lens = jnp.broadcast_to(lax.dynamic_index_in_dim(lengths, li, 0).astype(F32).reshape(1, 1), (8, 128))
    if inner:
        norm_in = jnp.pad(norm_low, ((0, 4), (0, 128 - R)))
    else:
        norm_in = jnp.pad(lax.all_gather(norm_master, "dp", axis=1, tiled=True), ((0, 4), (0, 0)))
        norm_in = norm_in.astype(BF16).astype(F32)
        full = lax.all_gather(pack, "dp", axis=1, tiled=True)
        every = lax.all_gather(full, "head", axis=0)
        pair = lax.dynamic_slice_in_dim(every, 2 * core, 2, 0)
        pack = jnp.concatenate([pair[0], pair[1]], axis=2)
    cos, sin_a, sin_b = rope_tables(T)

    hbm = pl.BlockSpec(memory_space=pl.ANY)
    vmem = pl.BlockSpec(memory_space=pltpu.VMEM)
    dma = pltpu.SemaphoreType.DMA
    quarter = T // 4
    g_shape = (3, R, 768) if inner else (3, D, 1536)
    out_shape = (
        jax.ShapeDtypeStruct((2, quarter, D), BF16),
        jax.ShapeDtypeStruct((2, quarter, D), BF16),
        jax.ShapeDtypeStruct(g_shape, F32 if inner else BF16),
        jax.ShapeDtypeStruct((8, D), F32),
        jax.ShapeDtypeStruct((8, 128), F32),
    )
    HALF = T // 2
    NB = T // 256
    bf = lambda *s: pltpu.VMEM(s, BF16)
    ff = lambda *s: pltpu.VMEM(s, F32)
    RC = 2 * R
    pieces = PIECES if inner else 1
    lx_rows = RC if inner else 16
    zl_rows = R if inner else 16
    scratch = [
        bf(3, D, 1536), bf(D, 1536), bf(T, D), bf(T, D), bf(D, T), bf(T, D), bf(D, T), bf(T, D), bf(D, T), ff(T, D),
        bf(6, T, 128), bf(6, T, 128), bf(6, T, 128), bf(6, T, 128), bf(3, 128, T),
        bf(3, T, 128), bf(3, T, 128), bf(2, T, 256), bf(2, D, 256), bf(T, 1536), bf(T, 1536), ff(T, D), bf(T, D), ff(128, T),
        bf(HALF, D), bf(HALF, D), bf(HALF, D), bf(HALF, D), bf(2, HALF, D),
        ff(8, 128), ff(8, D), ff(8, 8, 128), ff(8, 8, D), ff(4, 8, D), ff(8, 8, 128), ff(4, 8, 128),
        bf(pieces, 2, 2, lx_rows, SUB), bf(pieces, 2, lx_rows, SUB), bf(pieces, 4, zl_rows, SUB),
        dma((3,)), dma((3,)), dma((3,)), dma((3,)), dma((2,)), dma((2,)), dma((NB,)), dma((NB,)),
        dma((1,)), dma((1,)), dma((1,)), dma((1,)), dma((2, 2)), dma((2, 2)), dma((4,)), dma((4,)), dma((2, 11)), dma((2, 11)),
        dma((pieces, 4)), dma((pieces, 4)), dma((pieces, 2, 3)), dma((pieces, 2, 3)),
        dma((pieces, 2, 2)), dma((pieces, 2, 2)), dma((pieces, 2)), dma((pieces, 2)), dma((pieces, 4)), dma((pieces, 4)),
        dma((6,)),
    ]
    layer_out, input_grad, grads, gn, sq = pl.pallas_call(
        functools.partial(layer_kernel, inner, T, D, R),
        out_shape=out_shape,
        in_specs=[hbm, hbm, vmem, vmem if inner else hbm, vmem, vmem, vmem, vmem],
        out_specs=(hbm, hbm, vmem if inner else hbm, vmem, vmem),
        scratch_shapes=scratch,
        compiler_params=pltpu.CompilerParams(
            collective_id=0, has_side_effects=True, vmem_limit_bytes=63 * 2**20
        ),
        name="layer",
    )(inputs, cotangent, lens, pack, norm_in, jnp.asarray(cos), jnp.asarray(sin_a), jnp.asarray(sin_b))

    if inner:
        gn = gn[:4]
        squares = jnp.sum(sq)
    else:
        spread = jnp.stack([grads[:, :, :768], grads[:, :, 768:]]).astype(F32)
        empty = jnp.zeros((4,) + spread.shape[1:], F32)
        spread = lax.dynamic_update_slice_in_dim(empty, spread, 2 * core, 0)
        mine = lax.psum_scatter(spread, "head", scatter_dimension=0, tiled=False)
        grads = lax.psum_scatter(mine, "dp", scatter_dimension=1, tiled=True)
        gn = lax.psum(gn[:4], ("dp", "head"))
        squares = lax.psum(jnp.sum(grads * grads), ("dp", "head"))
    squares = squares + jnp.sum(gn * gn)
    gn_mine = lax.dynamic_slice_in_dim(gn, d * R, R, 1)
    a = grads[0]
    g_proj = jnp.stack([jnp.concatenate([a[:, 128 * j : 128 * j + 128], a[:, 384 + 64 * j : 448 + 64 * j]], axis=1) for j in range(3)])
    g_out = jnp.concatenate([a[:, 640:], a[:, 576:640]], axis=1).T
    g_up = grads[1]
    g_down = grads[2].T
    grad_norm = jnp.sqrt(squares)
    clip_factor = jnp.minimum(1.0, CLIP_LIMIT / (grad_norm + 1e-06))
    proj_up = adam_update(proj_master, proj_first, proj_second, g_proj, clip_factor, RATE_MATRIX, WEIGHT_DECAY)
    out_up = adam_update(out_master, out_first, out_second, g_out, clip_factor, RATE_MATRIX, WEIGHT_DECAY)
    up_up = adam_update(up_master, up_first, up_second, g_up, clip_factor, RATE_MATRIX, WEIGHT_DECAY)
    down_up = adam_update(down_master, down_first, down_second, g_down, clip_factor, RATE_MATRIX, WEIGHT_DECAY)
    norm_up = adam_update(norm_master, norm_first, norm_second, gn_mine, clip_factor, RATE_NORM, 0.0)
    return (layer_out, input_grad, grad_norm) + proj_up + out_up + up_up + down_up + norm_up


def solution(mesh):
    proj, wide, tall, norms = P(None, "dp", "head"), P("dp", "head"), P("head", "dp"), P(None, "dp")
    tokens = P("dp", None, None)
    placed = (tokens, tokens, P("dp")) + (proj,) * 3 + (tall,) * 3 + (wide,) * 3 + (tall,) * 3 + (norms,) * 3
    quarters = P("dp", "head", None)
    return jax.shard_map(
        per_device,
        mesh=mesh,
        in_specs=placed,
        out_specs=(quarters, quarters, P()) + (proj,) * 4 + (tall,) * 4 + (wide,) * 4 + (tall,) * 4 + (norms,) * 4,
        check_vma=False,
    )
```

time: 1060 us -> 255 us (0.24)
  waiting for transfers between devices: 643 us -> 0 us
  Pallas kernels: 0 us -> 228 us
  local copies, waits for them, and re-layouts: 119 us -> 8.98 us
  matrix products: 109 us -> 0 us
  blocking collectives: 74.4 us -> 0 us
  other arithmetic: 85.8 us -> 13.4 us
  between operations: 21.4 us -> 4.1 us
    psum x4 -> x0, waiting for transfers between devices: 584 us -> none  [the longest x1 213 us: per_device(): middle = rows_in + lax.psum(branch, 'head')]
    pallas_call x0 -> x1, Pallas kernels: none -> 228 us  [per_device(): pl.pallas_call(functools.partial(layer_kernel, inner, T, D, R), out_shape...]
    dot_general x38 -> x0, matrix products: 102 us -> none  [the longest x1 18.4 us: per_device(): upper_rows = jnp.dot(hidden_two, up_w, preferred_element_type=jnp.float32)]
    unnamed x14 -> x0, waiting for transfers between devices: 59.4 us -> none
    psum x1 -> x0, blocking collectives: 39.3 us -> none  [per_device(): total_squares = lax.psum(squares, ('dp', 'head'))]
    all_gather x3 -> x0, blocking collectives: 35.1 us -> none  [the longest x1 14.3 us: per_device(): lax.all_gather(lowered[0], 'dp', axis=1, tiled=True)]
    reduce_sum x15 -> x1, other arithmetic: 32.2 us -> 1.28 us  [per_device(): squares = jnp.sum(sq)]
    unnamed x120 -> x37, local copies, waits for them, and re-layouts: 34.3 us -> 5.92 us
  transfers between devices with their start and end apart: 11 -> 0, of which waited for: 5 -> 0; matrix products, arithmetic and copies ran while one was open for 18% -> 0% of each run, Pallas kernels for 0% -> 0%
where the time goes in v1:
time: 255 us; the launch traced here: 254 us
  Pallas kernels  228 us (89%)
  other arithmetic  13.4 us (5%)
  local copies, waits for them, and re-layouts  8.98 us (4%)
  between operations  4.1 us (2%)
    pallas_call x1, Pallas kernels, per_device(): pl.pallas_call(functools.partial(layer_kernel, inner, T, D, R), out_shape...  228 us
    convert_element_type x5, other arithmetic, adam_update(): return (master_new, first_new, second_new, master_new.astype(BF16))  6.36 us
    unnamed x37, local copies, waits for them, and re-layouts  5.92 us

profile of v1, /device:TPU:0, one launch (start us, length us, event | category | flops | bytes accessed | tf_op | source)
XLA Modules:
  0.0 254.5 jit_solution(11004923824928606981)
XLA Ops:
  0.7 0.0 copy-start.10
  0.7 1.2 dynamic_slice.7
  2.6 0.6 broadcast_in_dim.8.refs_2_
  3.2 1.0 convert.39
  4.2 1.0 copy.44
  5.2 0.1 concatenate.16
  5.3 1.0 convert_bitcast_fusion
  6.3 1.0 convert_bitcast_fusion.1
  7.3 0.8 pad_maximum_fusion.refs_3_
  8.1 0.0 copy-done.10
  8.1 0.6 pad_convert_fusion.refs_4_
  8.7 227.9 %layer.1 = (bf16[2,256,768]{2,1,0:T(8,128)(2,1)}, bf16[2,256,768]{2,1,0:T(8,128)(2,1)}, f32[3,96,768]{2,1,0:T(8,128)}, f32[8,768]{1,0:T(8,128)}, f32[8,128]{1,0:T(8,128)}) custom-call(bf16[2,1024,768]{2,1,0:T(8,128)(2,1)} %refs_0_.1, bf16[2,1024,768]{2,1,0:T(8,128)(2,1)} %refs_1_.1, f32[8,128]{1,0:T(8,128)} %broadcast_in_dim.8.refs_2_, ...), custom_call_target="tpu_custom_call" | custom-call | tf_op jit(solution)/shard_map/layer/pallas_call | solution.py:891
  236.7 0.0 copy-start.11
  236.7 0.0 copy-start.12
  236.7 0.0 copy-start.13
  236.7 0.0 copy-start.8
  236.7 0.0 copy-start.9
  236.7 1.4 fusion.22
  238.1 1.3 reduce_sum.18
  240.8 0.0 copy-done
  240.8 0.0 copy-done.5
  240.8 2.2 fusion.10
  243.0 0.0 copy-done.1
  243.0 2.3 fusion.13
  245.3 0.0 copy-done.11
  245.3 0.0 copy-done.12
  245.3 0.0 copy-done.13
  245.3 0.7 fusion.8
  246.0 1.0 slice_bitcast_fusion
  247.0 0.1 fusion.21
  247.1 0.0 copy-start.3
  247.1 0.0 copy-done.8
  247.1 0.1 copy.45
  247.2 0.0 copy-done.9
  247.2 0.1 copy.46
  247.3 0.1 fusion.16
  247.4 0.7 copy.49
  248.2 0.7 copy.50
  248.9 0.7 copy.51
  249.7 0.7 copy.52
  250.4 0.0 copy-done.2
  250.4 0.0 copy-done.6
  250.4 0.0 copy-done.7
  250.5 1.1 fusion.18
  251.6 0.0 copy-done.4
  251.6 0.9 copy.55
  252.4 0.0 copy-done.3
  252.4 0.9 copy.56
  (16 shorter events, 0.1 us)
Async XLA Ops:
  0.7 7.5 %copy-start.10 = (f32[4,96]{1,0:T(4,128)S(1)}, f32[4,96]{1,0:T(4,128)}, u32[]{:S(2)}) copy-start(f32[4,96]{1,0:T(4,128)} %param.36) | copy-start | bytes 4612
  8.7 232.1 %copy-start = (f32[768,96]{0,1:T(8,128)S(1)}, f32[768,96]{0,1:T(8,128)}, u32[]{:S(2)}) copy-start(f32[768,96]{0,1:T(8,128)} %param.33) | copy-start | bytes 884740
  8.7 232.1 %copy-start.5 = (f32[768,96]{0,1:T(8,128)S(1)}, f32[768,96]{0,1:T(8,128)}, u32[]{:S(2)}) copy-start(f32[768,96]{0,1:T(8,128)} %param.34) | copy-start | bytes 884740
  8.7 234.3 %copy-start.1 = (f32[96,768]{1,0:T(8,128)S(1)}, f32[96,768]{1,0:T(8,128)}, u32[]{:S(2)}) copy-start(f32[96,768]{1,0:T(8,128)} %param.30) | copy-start | bytes 884740
  236.7 8.6 %copy-start.11 = (f32[4,96]{1,0:T(4,128)S(1)}, f32[4,96]{1,0:T(4,128)}, u32[]{:S(2)}) copy-start(f32[4,96]{1,0:T(4,128)} %param.36) | copy-start | bytes 4612
  236.7 8.6 %copy-start.12 = (f32[4,96]{1,0:T(4,128)S(1)}, f32[4,96]{1,0:T(4,128)}, u32[]{:S(2)}) copy-start(f32[4,96]{1,0:T(4,128)} %param.37) | copy-start | bytes 4612
  236.7 8.6 %copy-start.13 = (f32[4,96]{1,0:T(4,128)S(1)}, f32[4,96]{1,0:T(4,128)}, u32[]{:S(2)}) copy-start(f32[4,96]{1,0:T(4,128)} %param.38) | copy-start | bytes 4612
  236.7 10.4 %copy-start.8 = (f32[192,96]{1,0:T(8,128)S(1)}, f32[192,96]{1,0:T(8,128)}, u32[]{:S(2)}) copy-start(f32[192,96]{1,0:T(8,128)} %param.28) | copy-start | bytes 221188
  236.7 10.5 %copy-start.9 = (f32[192,96]{1,0:T(8,128)S(1)}, f32[192,96]{1,0:T(8,128)}, u32[]{:S(2)}) copy-start(f32[192,96]{1,0:T(8,128)} %param.29) | copy-start | bytes 221188
  243.0 7.4 %copy-start.2 = (f32[3,96,192]{2,1,0:T(8,128)S(1)}, f32[3,96,192]{2,1,0:T(8,128)}, u32[]{:S(2)}) copy-start(f32[3,96,192]{2,1,0:T(8,128)} %param.24) | copy-start | bytes 663556
  243.0 7.5 %copy-start.6 = (f32[3,96,192]{2,1,0:T(8,128)S(1)}, f32[3,96,192]{2,1,0:T(8,128)}, u32[]{:S(2)}) copy-start(f32[3,96,192]{2,1,0:T(8,128)} %param.25) | copy-start | bytes 663556
  243.0 7.5 %copy-start.7 = (f32[3,96,192]{2,1,0:T(8,128)S(1)}, f32[3,96,192]{2,1,0:T(8,128)}, u32[]{:S(2)}) copy-start(f32[3,96,192]{2,1,0:T(8,128)} %param.26) | copy-start | bytes 663556
  245.3 6.2 %copy-start.4 = (bf16[2,256,768]{2,1,0:T(8,128)(2,1)S(1)}, bf16[2,256,768]{2,1,0:T(8,128)(2,1)}, u32[]{:S(2)}) copy-start(bf16[2,256,768]{2,1,0:T(8,128)(2,1)} %get-tuple-element.117) | copy-start | bytes 2359300
  247.1 5.3 %copy-start.3 = (bf16[2,256,768]{2,1,0:T(8,128)(2,1)S(1)}, bf16[2,256,768]{2,1,0:T(8,128)(2,1)}, u32[]{:S(2)}) copy-start(bf16[2,256,768]{2,1,0:T(8,128)(2,1)} %get-tuple-element.118) | copy-start | bytes 2359300

commit v2 on v1

v2 whole, which is shorter than its diff:
```python
import functools

import jax
import jax.numpy as jnp
import numpy as np
from jax import lax
from jax.experimental import pallas as pl
from jax.experimental.pallas import tpu as pltpu
from jax.sharding import PartitionSpec as P

HD = 64
STEP = 5
LN_EPSILON = 1e-05
MASK_FILL = -1e30
ROPE_BASE = 10000.0
CLIP_LIMIT = 1.0
BETA_FIRST = 0.9
BETA_SECOND = 0.95
ADAM_EPSILON = 1e-08
WEIGHT_DECAY = 0.1
RATE_MATRIX = 0.03
RATE_NORM = 0.3
INV_ROOT_TWO = 0.7071067811865476
INV_ROOT_TWO_PI = 0.3989422804014327

F32 = jnp.float32
BF16 = jnp.bfloat16
MESH = pl.DeviceIdType.MESH
SUB = 256
PIECES = 9


def dot(a, b):
    return lax.dot_general(a, b, (((1,), (0,)), ((), ())), preferred_element_type=F32)


def dot_t(a, b):
    return lax.dot_general(a, b, (((1,), (1,)), ((), ())), preferred_element_type=F32)


def row_mean(v):
    return jnp.mean(v, axis=-1, keepdims=True)


def normalize(v):
    center = v - row_mean(v)
    inverse = lax.rsqrt(row_mean(center * center) + LN_EPSILON)
    return center * inverse, inverse


def lanes(rows):
    return lax.broadcasted_iota(jnp.int32, (rows, 128), 1)


def head_lanes(lane, half):
    return lane < HD if half == 0 else lane >= HD


def three_parts(col):
    hi = col.astype(BF16).astype(F32)
    mid = (col - hi).astype(BF16).astype(F32)
    return hi, mid, col - hi - mid


def spare_columns(lane, base, values, other):
    out = other
    for i, v in reversed(list(enumerate(values))):
        out = jnp.where(lane == base + i, v, out)
    return out


def turned(v, first):
    return jnp.where(first, pltpu.roll(v, 96, 1), pltpu.roll(v, 32, 1))


def rope(v, cos, sin, first):
    return v * cos + turned(v, first) * sin


def rope_back(v, cos, sin, first):
    return v * cos - turned(v, first) * sin


def run(name, count, body):
    with jax.named_scope(name):
        lax.fori_loop(0, count, body, 0)


def layer_kernel(inner, T, D, R, *refs):
    (
        x_in, ct_in, lens_in, tables_in, norm_in, *rest
    ) = refs
    if inner:
        *masters_in, lo_out, ig_out, g_out, small_out = rest[:8]
        rest = rest[8:]
    else:
        w_in, lo_out, ig_out, g_out, small_out = rest[:5]
        rest = rest[5:]
    (
        W, GA, xs, cc, cT, h1, h1T, h2, h2T, x1, qe, ke, ve, doe, kT,
        opair, osib, wsib, zb, du, dh2, dh2r, dqT, facc, fsend, frecv, drecv, stage,
        lens_s, lens_v, pack, nw, nl, gl1, gl2, sl1, sl2, LX, LY, ZL,
        in_s, in_r, o_s, o_r, ws_s, ws_r, d2_s, d2_r, f_s, f_r, d1_s, d1_r, out_s, out_r, n_s, n_r, e_s, e_r,
        s1s, s1r, a2s, a2r, r1s, r1r, r2s, r2r, zss, zsr, loc,
        tables, norm_m, proj_m, out_m, up_m, down_m, gn_out, sq_out, gbuf, squares_ref,
    ) = rest
    RC = 2 * R
    TB = 256
    NB = T // TB
    HALF = T // 2
    d = lax.axis_index("dp")
    z = lax.axis_index("head")
    core = d % 2
    k = d // 2
    own = z // 2
    li = z % 2
    sib = (d + 1 - 2 * core, z)
    master_copies = []
    if inner:
        for i, (src, dst) in enumerate(zip(masters_in, (proj_m, out_m, up_m, down_m))):
            master_copies.append(pltpu.make_async_copy(src, dst, loc.at[4 + i]))
    norm_copy = pltpu.make_async_copy(norm_in, norm_m, loc.at[8])
    table_copy = pltpu.make_async_copy(tables_in, tables, loc.at[9])
    for copy in master_copies + [norm_copy, table_copy]:
        copy.start()
    cos_ref, sin_ref = tables.at[0], tables.at[1]
    lens_s[...] = jnp.full((8, 128), lens_in[li].astype(F32))

    def rc(src, dst, ss, rs, dev):
        return pltpu.make_async_remote_copy(
            src_ref=src, dst_ref=dst, send_sem=ss, recv_sem=rs, device_id=dev, device_id_type=MESH
        )

    column = []
    for da in range(2):
        for dz in range(4):
            if da + dz > 0:
                dd = d if da == 0 else sib[0]
                column.append((da * 4 + dz, (dd, (z + dz) % 4)))
    if inner:
        kx = k + 1 - 2 * (k % 2)
        ky = (k + 2) % 4
        kd = 3 - k
        xdev = (2 * kx + core, z)
        ydev = (2 * ky + core, z)
        ddev = (2 * kd + core, z)
        plane = [xdev, ydev, ddev]
    else:
        plane = []
    everyone = [dev for _, dev in column] + plane
    barrier = pltpu.get_barrier_semaphore()
    for dev in everyone:
        pl.semaphore_signal(barrier, inc=1, device_id=dev, device_id_type=MESH)
    pl.semaphore_wait(barrier, len(everyone))

    def in_remote(i):
        src = (x_in.at[li], ct_in.at[li], lens_s)[i]
        dst = (xs, cc, lens_v)[i]
        return rc(src, dst, in_s.at[i], in_r.at[i], sib)

    def in_local(i):
        src = (x_in.at[li], ct_in.at[li], lens_s)[i]
        dst = (xs, cc, lens_v)[i]
        return pltpu.make_async_copy(src, dst, loc.at[i])

    @pl.when(core == own)
    def _():
        for i in (2, 0, 1):
            in_remote(i).start()
            in_local(i).start()

    def piece(s):
        if isinstance(s, int):
            if s < 3:
                return 0, SUB * s
            return 1 + (s - 3) % 2, SUB * ((s - 3) // 2)
        return 1 + (s - 3) % 2, pl.multiple_of(((s - 3) // 2) * SUB, SUB)

    def rows_at(block, size):
        return pl.ds(pl.multiple_of(block * size, 16), size)

    def cols_at(e, col):
        if isinstance(e, int) and isinstance(col, int):
            return pl.ds(e * 768 + col, SUB)
        return pl.ds(pl.multiple_of(e * 768 + col, 128), SUB)

    def ag1(s, dz, a, e, dev):
        j, col = piece(s)
        src = pack.at[j, :, pl.ds(col, SUB)]
        dst = W.at[j, rows_at(2 * k + a, R), cols_at(e, col)]
        return rc(src, dst, s1s.at[s, dz], s1r.at[s, a * 2 + e], dev)

    def ag1_start(s):
        j, col = piece(s)
        for dz in range(1, 4):
            ag1(s, dz, core, li, (2 * k + own, (z + dz) % 4)).start()

        @pl.when(core == own)
        def _():
            pltpu.make_async_copy(
                pack.at[j, :, pl.ds(col, SUB)], W.at[j, rows_at(d, R), cols_at(li, col)], s1r.at[s, core * 2 + li]
            ).start()

        @pl.when(core != own)
        def _():
            ag1(s, 0, core, li, sib).start()

    def ag2(s, e, to, rows, dev, slot):
        j, col = piece(s)
        region = W.at[j, rows_at(rows, RC), cols_at(e, col)]
        return rc(region, region, a2s.at[s, e, to], a2r.at[s, e, slot], dev)

    def ag2_start(s):
        for a in range(2):
            for e in range(2):
                ag1(s, 1, a, e, sib).wait_recv()
        for e in range(2):
            ag2(s, e, 0, k, xdev, 0).start()
            ag2(s, e, 1, k, ydev, 1).start()

    def ag3_start(s):
        ag2(s, 0, 2, kx, ydev, 0).wait_recv()
        ag2(s, 0, 2, kx, ydev, 2).start()
        ag2(s, 1, 2, ky, xdev, 1).wait_recv()
        ag2(s, 1, 2, ky, xdev, 2).start()

    def ag_wait(s):
        ag2(s, 0, 1, ky, ydev, 1).wait_recv()
        ag2(s, 0, 2, kd, ydev, 2).wait_recv()
        ag2(s, 1, 0, kx, xdev, 0).wait_recv()
        ag2(s, 1, 2, kd, xdev, 2).wait_recv()

    def ag_drain(s):
        for dz in range(1, 4):
            ag1(s, dz, core, li, sib).wait_send()

        @pl.when(core != own)
        def _():
            ag1(s, 0, core, li, sib).wait_send()

        for e in range(2):
            for to in range(3):
                ag2(s, e, to, k, xdev, to).wait_send()

    if inner:
        for copy in master_copies[:2]:
            copy.wait()
        out_t = jnp.concatenate([out_m[...], jnp.zeros((192, 128 - R), F32)], axis=1).T[:R]
        tail_q, tail_k, tail_v = (proj_m[j, :, 128:192] for j in range(3))
        for j in range(3):
            pack[0, :, 128 * j : 128 * j + 128] = proj_m[j, :, :128].astype(BF16)
        pack[0, :, 384:512] = jnp.concatenate([tail_q, tail_k], axis=1).astype(BF16)
        pack[0, :, 512:640] = jnp.concatenate([tail_v, out_t[:, 128:]], axis=1).astype(BF16)
        pack[0, :, 640:768] = out_t[:, :128].astype(BF16)
        for s in range(3):
            ag1_start(s)
        norm_copy.wait()
        nl[pl.ds(d, 1)] = jnp.zeros((1, 8, 128), F32)
        nl[pl.ds(d, 1), 0:4, 0:R] = norm_m[...].astype(BF16).astype(F32).reshape(1, 4, R)
        rc(nl.at[pl.ds(d, 1)], nl.at[pl.ds(d, 1)], n_s.at[0], n_r.at[0], sib).start()
        for copy in master_copies[2:]:
            copy.wait()
        pack[1] = up_m[...].astype(BF16)
        pack[2] = down_m[...].astype(BF16)
        for s in range(3, PIECES):
            ag1_start(s)
        rc(nl.at[pl.ds(d, 1)], nl.at[pl.ds(sib[0], 1)], n_s.at[0], n_r.at[0], sib).wait()
        for i, dev in enumerate(plane):
            rc(nl.at[pl.ds(2 * k, 2)], nl.at[pl.ds(2 * k, 2)], n_s.at[1 + i], n_r.at[1 + i], dev).start()
        ag2_start(0)
    else:
        w_copy = pltpu.make_async_copy(w_in, W, loc.at[3])
        w_copy.start()

    @pl.when(core == own)
    def _():
        for i in range(3):
            in_local(i).wait()

    @pl.when(core != own)
    def _():
        for i in range(3):
            in_remote(i).wait_recv()

    if inner:
        for i, kk in enumerate((kx, ky, kd)):
            rc(nl.at[pl.ds(2 * kk, 2)], nl.at[pl.ds(2 * kk, 2)], n_s.at[1 + i], n_r.at[1 + i], plane[i]).wait()
        nw[...] = jnp.concatenate([nl[i][:, :R] for i in range(8)], axis=1)
    else:
        norm_copy.wait()
        nw[...] = norm_m[...]

    length = lens_v[0:1, 0:1]

    def row_valid(start, rows):
        ids = (lax.broadcasted_iota(jnp.int32, (rows, 1), 0) + start).astype(F32)
        return ids < length

    def at(i, size=TB):
        return pl.ds(pl.multiple_of(i * size, size), size)

    def norm_one(i, carry):
        rows = at(i)
        n, _ = normalize(xs[rows, :].astype(F32))
        h = (n * nw[0:1, :] + nw[1:2, :]).astype(BF16)
        h1[rows, :] = h
        h1T[:, rows] = h.T
        return carry

    def mask_cotangent(i, carry):
        rows = at(i)
        c = jnp.where(row_valid(i * TB, TB), cc[rows, :].astype(F32), 0.0).astype(BF16)
        cc[rows, :] = c
        cT[:, rows] = c.T
        return carry

    if inner:
        ag2_start(1)
        ag3_start(0)
    run("norm_one", NB // 2, norm_one)
    if inner:
        ag2_start(2)
    run("norm_one", NB // 2, lambda i, carry: norm_one(i + NB // 2, carry))
    if inner:
        ag3_start(1)
    else:
        w_copy.wait()
    run("mask_cotangent", NB, mask_cotangent)
    table_copy.wait()
    if inner:
        ag_wait(0)
        ag3_start(2)
        ag2_start(3)
        ag_wait(1)
        ag2_start(4)

    lane = lanes(TB)
    low = lane < HD
    first = lane % HD < HD // 2

    def make_pair(p):
        def block(i, carry):
            rows = at(i)
            h = h1[rows, :]
            cos, sin = cos_ref[rows, :], sin_ref[rows, :]
            if p < 2:
                raw = dot(h, W[0, :, p * 768 : p * 768 + 384])
                q, kk, v = raw[:, :128], raw[:, 128:256], raw[:, 256:]
                q = rope(q, cos, sin, first)
                kk = rope(kk, cos, sin, first)
            else:
                r0 = dot(h, W[0, :, 384:640])
                r1 = dot(h, W[0, :, 768 + 384 : 768 + 640])
                ra = rope(r0[:, :128], cos, sin, first)
                rb = rope(r1[:, :128], cos, sin, first)
                q = jnp.where(low, ra, pltpu.roll(rb, 64, 1))
                kk = jnp.where(low, pltpu.roll(ra, 64, 1), rb)
                v = jnp.where(low, r0[:, 128:], pltpu.roll(r1[:, 128:], 64, 1))
            q = q * HD**-0.5
            bias = jnp.where(row_valid(i * TB, TB), 0.0, MASK_FILL)
            kT[p, :, rows] = kk.astype(BF16).T
            for half in range(2):
                mine = head_lanes(lane, half)
                base = HD - HD * half
                hh = 2 * p + half
                qe[hh, rows, :] = jnp.where(mine, q, jnp.where(lane == base, 1.0, 0.0)).astype(BF16)
                ke[hh, rows, :] = jnp.where(mine, kk, jnp.where(lane == base, bias, 1.0)).astype(BF16)
                ve[hh, rows, :] = jnp.where(mine, v, 1.0).astype(BF16)
            return carry

        run("make_pair", NB, block)

    def attend(p, i):
        rows = at(i)
        outs = []
        for half in range(2):
            hh = 2 * p + half
            mine = head_lanes(lane, half)
            base = HD - HD * half
            q = qe[hh, rows, :]
            s = dot_t(q, ke[hh])
            top = jnp.max(s, axis=-1, keepdims=True)
            ex = jnp.exp(s - top).astype(BF16)
            o = dot(ex, ve[hh])
            total = o[:, base : base + 1]
            outs.append(o * (1.0 / total))
            hi, mid, lo = three_parts(top + jnp.log(total))
            extra = spare_columns(lane, base, (1.0, -hi, -mid, -lo), 0.0)
            qe[hh, rows, :] = jnp.where(mine, q.astype(F32), extra).astype(BF16)
        opair[p, rows, :] = jnp.where(low, outs[0], outs[1]).astype(BF16)

    def o_copy(p):
        return rc(opair.at[p], osib.at[p], o_s.at[p], o_r.at[p], sib)

    def ws_copy(e):
        return rc(W.at[0, :, pl.ds(e * 768 + 512, 256)], wsib.at[e], ws_s.at[e], ws_r.at[e], sib)

    for p in range(3):
        if inner and p == 1:
            ag3_start(3)
        if inner and p == 2:
            ag_wait(2)
            ag2_start(8)
        make_pair(p)

        def attend_two(i, carry, p=p):
            attend(p, 2 * i)
            if inner and p == 0:
                ag2_start(5 + i)
            if inner and p == 1:
                pl.when(i == 0)(lambda: ag2_start(7))
                pl.when(i == 1)(lambda: ag3_start(4))
            if inner and p == 2:
                pl.when(i == 0)(lambda: ag3_start(5))
            attend(p, 2 * i + 1)
            return carry

        run("attend_two", NB // 2, attend_two)
        o_copy(p).start()
        if p == 2:
            for e in range(2):
                ws_copy(e).start()

    def wide_o(pairs, e, rows):
        single = pairs[2, rows, :].astype(F32)
        if e == 0:
            single = pltpu.roll(single, 64, 1)
        single = jnp.where(low, 0.0, single).astype(BF16)
        return jnp.concatenate([single, pairs[e, rows, :]], axis=1)

    for p in range(3):
        o_copy(p).wait()
    for e in range(2):
        ws_copy(e).wait()
    if inner:
        ag3_start(6)

    def project_out(i, carry):
        rows = at(i)
        acc = xs[rows, :].astype(F32)
        for e in range(2):
            acc = acc + dot_t(wide_o(opair, e, rows), W[0, :, e * 768 + 512 : e * 768 + 768])
            acc = acc + dot_t(wide_o(osib, e, rows), wsib[e])
        x1[rows, :] = acc
        n, _ = normalize(acc)
        h = (n * nw[2:3, :] + nw[3:4, :]).astype(BF16)
        h2[rows, :] = h
        h2T[:, rows] = h.T
        return carry

    run("project_out", NB, project_out)
    if inner:
        ag3_start(7)

    def grad(s):
        return GA if isinstance(s, int) and s < 3 else W.at[piece(s)[0]]

    def ways(s, e):
        flip = isinstance(s, int) and s == 1
        one, two = ((kx, xdev), (ky, ydev)) if e == int(flip) else ((ky, ydev), (kx, xdev))
        return one, two

    def rs1(s, e, b, rows, dev):
        src = grad(s).at[rows_at(rows, RC), cols_at(e, piece(s)[1])]
        return rc(src, LX.at[s, e, b], r1s.at[s, e, b], r1r.at[s, e, b], dev)

    def rs1_half(s, e):
        (near, dev), _ = ways(s, e)
        rs1(s, e, 1, kd, dev).start()
        rs1(s, e, 0, near, dev).start()

    def rs2(s, e, dev):
        return rc(LX.at[s, e, 1], LY.at[s, e], r2s.at[s, e], r2r.at[s, e], dev)

    def rs2_half(s, e):
        _, (far, dev) = ways(s, e)
        rs1(s, e, 1, far, dev).wait_recv()
        mine = grad(s)[rows_at(far, RC), cols_at(e, piece(s)[1])].astype(F32)
        LX[s, e, 1] = (LX[s, e, 1].astype(F32) + mine).astype(BF16)
        rs2(s, e, dev).start()

    def rs3(s, e, a, dev):
        return rc(LX.at[s, e, 0, pl.ds(a * R, R)], ZL.at[s, z], zss.at[s, e * 2 + a], zsr.at[s, z], dev)

    def rs3_half(s, e):
        rs1(s, e, 0, k, xdev).wait_recv()
        rs2(s, e, ydev).wait_recv()
        mine = grad(s)[rows_at(k, RC), cols_at(e, piece(s)[1])].astype(F32)
        LX[s, e, 0] = (LX[s, e, 0].astype(F32) + LY[s, e].astype(F32) + mine).astype(BF16)
        zt = 2 * core + e
        for a in range(2):
            here = (core == a) & (zt == z)

            @pl.when(here)
            def _(a=a, e=e):
                pltpu.make_async_copy(LX.at[s, e, 0, pl.ds(a * R, R)], ZL.at[s, z], zsr.at[s, z]).start()

            @pl.when(jnp.logical_not(here))
            def _(a=a, e=e, zt=zt):
                rs3(s, e, a, (2 * k + a, zt)).start()

    def rs1_start(s):
        for e in range(2):
            rs1_half(s, e)

    def rs2_start(s):
        for e in range(2):
            rs2_half(s, e)

    def rs3_start(s):
        for e in range(2):
            rs3_half(s, e)

    def rs4(s):
        j, col = piece(s)
        total = jnp.zeros((R, SUB), F32)
        for zz in range(4):
            rc(LX.at[s, 0, 0, pl.ds(0, R)], ZL.at[s, zz], zss.at[s, 0], zsr.at[s, zz], sib).wait_recv()
            total = total + ZL[s, zz].astype(F32)
        gbuf[j, :, pl.ds(col, SUB)] = total
        pltpu.make_async_copy(gbuf.at[j, :, pl.ds(col, SUB)], g_out.at[j, :, pl.ds(col, SUB)], loc.at[10]).start()
        return total

    def rs_drain(s):
        for e in range(2):
            for b in range(2):
                rs1(s, e, b, k, xdev).wait_send()
            rs2(s, e, ydev).wait_send()
            zt = 2 * core + e
            for a in range(2):

                @pl.when(jnp.logical_not((core == a) & (zt == z)))
                def _(a=a, e=e):
                    rs3(s, e, a, sib).wait_send()

    def out_copy(ref, which, qi, slot):
        src = stage.at[which, pl.ds(pl.multiple_of(qi * (T // 4), T // 4), T // 4), :]
        return rc(src, ref.at[li], out_s.at[which, qi], out_r.at[which, slot], (2 * k + own, 2 * core + qi))

    def out_start(ref, which, qi):
        here = (core == own) & (li == qi)

        @pl.when(here)
        def _():
            src = stage.at[which, pl.ds(pl.multiple_of(qi * (T // 4), T // 4), T // 4), :]
            pltpu.make_async_copy(src, ref.at[li], out_r.at[which, li]).start()

        @pl.when(jnp.logical_not(here))
        def _():
            out_copy(ref, which, qi, li).start()

    def out_wait(ref, which):
        for slot in range(2):
            src = stage.at[which, pl.ds(0, T // 4), :]
            rc(src, ref.at[slot], out_s.at[which, 0], out_r.at[which, slot], sib).wait_recv()
        for qi in range(2):

            @pl.when(jnp.logical_not((core == own) & (li == qi)))
            def _(qi=qi):
                out_copy(ref, which, qi, 0).wait_send()

    def d2_copy(i):
        return rc(h1.at[at(i), :], dh2r.at[at(i), :], d2_s.at[i], d2_r.at[i], sib)

    if inner:
        for s in range(3):
            ag_drain(s)

    for i3 in range(3):
        if inner:
            ag_wait(3 + 2 * i3)
            ag_wait(4 + 2 * i3)
        wide_cols = [cols_at(e, SUB * i3) for e in range(2)]

        def hidden(i, carry, i3=i3):
            rows = at(i % NB)
            e = i // NB
            cols = cols_at(e, SUB * i3)
            here = pl.ds(pl.multiple_of(e * SUB, SUB), SUB)
            u = dot(h2[rows, :], W[1, :, cols])
            dz = dot(cc[rows, :], W[2, :, cols])
            cumulative = 0.5 * (1.0 + lax.erf(u * INV_ROOT_TWO))
            slope = cumulative + u * jnp.exp(-0.5 * u * u) * INV_ROOT_TWO_PI
            zb[rows, here] = (u * cumulative).astype(BF16)
            du[rows, here] = (dz * slope).astype(BF16)
            return carry

        run("hidden", 2 * NB, hidden)
        if inner and i3 == 0:
            ag3_start(8)
        if inner and i3 == 2:
            rs2_start(3)

        def back_two(i, carry, i3=i3, wide_cols=wide_cols):
            rows = at(i)
            v = dot_t(du[rows, 0:SUB], W[1, :, wide_cols[0]]) + dot_t(du[rows, SUB : 2 * SUB], W[1, :, wide_cols[1]])
            f = dot_t(zb[rows, 0:SUB], W[2, :, wide_cols[0]]) + dot_t(zb[rows, SUB : 2 * SUB], W[2, :, wide_cols[1]])
            if i3 > 0:
                v = v + dh2[rows, :]
                f = f + facc[rows, :]
            dh2[rows, :] = v
            facc[rows, :] = f
            if i3 == 2:
                h1[rows, :] = v.astype(BF16)
                d2_copy(i).start()
            return carry

        run("back_two", NB, back_two)
        if inner:
            ag_drain(3 + 2 * i3)
            ag_drain(4 + 2 * i3)

        def grad_ffn(e, carry, i3=i3):
            here = pl.ds(pl.multiple_of(e * SUB, SUB), SUB)
            W[1, :, cols_at(e, SUB * i3)] = dot(h2T[...], du[:, here]).astype(BF16)
            W[2, :, cols_at(e, SUB * i3)] = dot(cT[...], zb[:, here]).astype(BF16)
            return carry

        run("grad_ffn", 2, grad_ffn)
        if inner:
            rs1_start(3 + 2 * i3)
            rs1_start(4 + 2 * i3)

    other = 1 - core

    def half_rows(which, i):
        return pl.ds(pl.multiple_of(which * HALF + i * TB, TB), TB)

    def f_copy():
        return rc(fsend, frecv, f_s.at[0], f_r.at[0], sib)

    def ffn_other(i, carry):
        fsend[at(i), :] = facc[half_rows(other, i), :].astype(BF16)
        return carry

    run("ffn_other", NB // 2, ffn_other)
    f_copy().start()
    f_copy().wait()

    def ffn_final(i, carry):
        rows = half_rows(core, i)
        y = x1[rows, :] + facc[rows, :] + frecv[at(i), :].astype(F32)
        stage[0, at(i), :] = y.astype(BF16)
        out_start(lo_out, 0, i)
        return carry

    run("ffn_final", NB // 2, ffn_final)

    gn_out[...] = jnp.zeros_like(gn_out)

    def norm_back_two(i, carry):
        rows = at(i)
        d2_copy(i).wait()
        e2 = dh2[rows, :] + dh2r[rows, :].astype(F32)
        n, r = normalize(x1[rows, :])
        m = e2 * nw[2:3, :]
        dx = cc[rows, :].astype(F32) + r * (m - row_mean(m) - n * row_mean(m * n))
        dh2[rows, :] = dx
        low_dx = dx.astype(BF16)
        h2[rows, :] = low_dx
        h2T[:, rows] = low_dx.T
        count = jnp.where(i // (NB // 2) == core, 1.0, 0.0)
        gn_out[2:3, :] += count * jnp.sum(e2 * n, axis=0, keepdims=True)
        gn_out[3:4, :] += count * jnp.sum(e2, axis=0, keepdims=True)
        return carry

    run("norm_back_two", NB, norm_back_two)
    da, daT = h2, h2T
    if inner:
        rs2_start(4)
        rs3_start(3)

    def do_block(i, carry):
        rows = at(i)
        for e in range(2):
            zb[rows, e * 256 : e * 256 + 256] = wide_o(opair, e, rows)
        parts = [dot(da[rows, :], W[0, :, e * 768 + 512 : e * 768 + 768]) for e in range(2)]
        pairs = [parts[0][:, 128:], parts[1][:, 128:], jnp.where(low, pltpu.roll(parts[0][:, :128], 64, 1), parts[1][:, :128])]
        for p in range(3):
            g = pairs[p].astype(BF16).astype(F32)
            prod = g * opair[p, rows, :].astype(F32)
            for half in range(2):
                mine = head_lanes(lane, half)
                base = HD - HD * half
                delta = jnp.sum(jnp.where(mine, prod, 0.0), axis=-1, keepdims=True)
                hi, mid, lo = three_parts(delta)
                extra = spare_columns(lane, base + 1, (-hi, -mid, -lo), 0.0)
                doe[2 * p + half, rows, :] = jnp.where(mine, g, extra).astype(BF16)
        return carry

    run("do_block", NB, do_block)
    if inner:
        rs2_start(5)
        rs2_start(6)

    def back_keys(p, i):
        rows = at(i)
        cos, sin = cos_ref[rows, :], sin_ref[rows, :]
        dks, dvs = [], []
        for half in range(2):
            hh = 2 * p + half
            sT = dot_t(ke[hh, rows, :], qe[hh])
            pT = jnp.exp(sT)
            dpT = dot_t(ve[hh, rows, :], doe[hh])
            dsT = (pT * dpT).astype(BF16)
            dvs.append(dot(pT.astype(BF16), doe[hh]))
            dks.append(dot(dsT, qe[hh]))
            part = dot(kT[p, half * HD : half * HD + HD, rows], dsT)
            dqT[half * HD : half * HD + HD, :] += part
        dk = rope_back(jnp.where(low, dks[0], dks[1]), cos, sin, first)
        dv = jnp.where(low, dvs[0], dvs[1])
        put_draw(p, rows, None, dk, dv)

    def put_draw(p, rows, dq, dk, dv):
        if p < 2:
            for i, v in enumerate((dq, dk, dv)):
                if v is not None:
                    du[rows, p * 768 + 128 * i : p * 768 + 128 * i + 128] = v.astype(BF16)
            return
        if dk is not None:
            du[rows, 640:768] = dk.astype(BF16)
            du[rows, 512:640] = jnp.where(low, dv, 0.0).astype(BF16)
            du[rows, 768 + 512 : 768 + 640] = jnp.where(low, pltpu.roll(dv, 64, 1), 0.0).astype(BF16)
        if dq is not None:
            dk = du[rows, 640:768].astype(F32)
            du[rows, 384:512] = jnp.where(low, dq, pltpu.roll(dk, 64, 1)).astype(BF16)
            du[rows, 768 + 384 : 768 + 512] = jnp.where(low, pltpu.roll(dq, 64, 1), dk).astype(BF16)

    def put_queries(p):
        def block(i, carry):
            rows = at(i)
            cos, sin = cos_ref[rows, :], sin_ref[rows, :]
            dq = dqT[:, rows].T * HD**-0.5
            put_draw(p, rows, rope_back(dq, cos, sin, first), None, None)
            return carry

        run("put_queries", NB, block)

    def back_pair(p, pumps):
        dqT[...] = jnp.zeros_like(dqT)

        def pump(i, half):
            if inner:
                for step in range(NB // 2):
                    if 2 * step + half in pumps:
                        pl.when(i == step)(pumps[2 * step + half])

        def back_step(i, carry):
            back_keys(p, 2 * i)
            pump(i, 0)
            back_keys(p, 2 * i + 1)
            pump(i, 1)
            return carry

        run("back_step", NB // 2, back_step)
        put_queries(p)

    def several(*steps):
        def go():
            for f, *of in steps:
                f(*of)

        return go

    back_pair(2, {1: several((rs2_start, 7)), 3: several((rs2_start, 8), (rs3_start, 4))})

    def grad_attn_two(e, carry):
        b = e * 768
        for col in (384, 512):
            here = pl.ds(pl.multiple_of(b + col, 128), 128)
            v = dot(h1T[...], du[:, here])
            if col == 512:
                wide = dot(daT[...], zb[:, pl.ds(pl.multiple_of(e * 256, 256), 256)])
                GA[:, pl.ds(pl.multiple_of(b + 640, 128), 128)] = wide[:, 128:].astype(BF16)
                v = v + wide[:, :128]
            GA[:, here] = v.astype(BF16)
        return carry

    run("grad_attn", 2, grad_attn_two)
    if inner:
        rs1_start(2)
        rs3_start(5)

    def grad_attn(p):
        def one(i, carry, b=p * 768):
            GA[:, b : b + 384] = dot(h1T[...], du[:, b : b + 384]).astype(BF16)
            return carry

        run("grad_attn", 1, one)

    back_pair(0, {0: several((rs3_start, 6)), 2: several((rs3_start, 7)), 3: several((rs3_start, 8))})
    grad_attn(0)
    squares_ref[...] = jnp.zeros_like(squares_ref)

    def four(s):
        g = rs4(s)
        squares_ref[...] += g * g

    if inner:
        rs1_half(0, 0)
        rs1_half(1, 0)
    back_pair(1, {0: several((rs2_start, 2)), 3: several((rs2_half, 0, 0), (rs2_half, 1, 0), (rs3_start, 2))})
    grad_attn(1)
    if inner:
        rs1_half(0, 1)
        rs1_half(1, 1)

    def back_one(rows):
        return dot_t(du[rows, 0:640], W[0, :, 0:640]) + dot_t(du[rows, 768 : 768 + 640], W[0, :, 768 : 768 + 640])

    def d1_copy(i):
        return rc(fsend.at[at(i), :], drecv.at[at(i), :], d1_s.at[i], d1_r.at[i], sib)

    def one_other(i, carry):
        fsend[at(i), :] = back_one(half_rows(other, i)).astype(BF16)
        d1_copy(i).start()
        return carry

    run("one_other", NB // 2, one_other)

    def one_mine(i, carry):
        rows = half_rows(core, i)
        x1[rows, :] = back_one(rows)
        return carry

    run("one_mine", NB // 2, one_mine)
    if inner:
        rs3_half(0, 0)
        rs3_half(1, 0)

    def norm_back_one(i, carry):
        rows = half_rows(core, i)
        d1_copy(i).wait()
        e1 = x1[rows, :] + drecv[at(i), :].astype(F32)
        n, r = normalize(xs[rows, :].astype(F32))
        m = e1 * nw[0:1, :]
        dx = dh2[rows, :] + r * (m - row_mean(m) - n * row_mean(m * n))
        stage[1, at(i), :] = dx.astype(BF16)
        gn_out[0:1, :] += jnp.sum(e1 * n, axis=0, keepdims=True)
        gn_out[1:2, :] += jnp.sum(e1, axis=0, keepdims=True)
        return carry

    run("norm_back_one", 1, norm_back_one)
    out_start(ig_out, 1, 0)
    run("norm_back_one", NB // 2 - 1, lambda i, carry: norm_back_one(i + 1, carry))

    def sum_first(l1, which):
        return [rc(l1.at[0], l1.at[slot], e_s.at[which, slot], e_r.at[which, slot], dev) for slot, dev in column]

    def sum_plane(l2, which):
        return [rc(l2.at[0], l2.at[1 + i], e_s.at[which, 8 + i], e_r.at[which, 8 + i], dev) for i, dev in enumerate(plane)]

    def sum_start(ref, l1, l2, which):
        l1[0] = ref[...]
        for copy in sum_first(l1, which):
            copy.start()

    def sum_second(l1, l2, which):
        for copy in sum_first(l1, which):
            copy.wait()
        total = l1[0]
        for slot in range(1, 8):
            total = total + l1[slot]
        l2[0] = total
        for copy in sum_plane(l2, which):
            copy.start()

    def sum_end(ref, l1, l2, which):
        for copy in sum_plane(l2, which):
            copy.wait()
        total = l2[0]
        for i in range(1, 4):
            total = total + l2[i]
        ref[...] = total

    if inner:
        sum_start(gn_out, gl1, gl2, 0)
        rs2_half(0, 1)
        rs2_half(1, 1)
        for s in range(3, PIECES):
            four(s)
        rs3_half(0, 1)
        rs3_half(1, 1)
    out_start(ig_out, 1, 1)
    if inner:
        sum_second(gl1, gl2, 0)
        four(2)
        sum_end(gn_out, gl1, gl2, 0)
        four(0)
        four(1)
        total = jnp.sum(squares_ref[...], axis=0, keepdims=True)
        total = total[:, :128] + total[:, 128:]
        sq_out[...] = jnp.where(lax.broadcasted_iota(jnp.int32, (8, 128), 0) == 0, total, 0.0)
        sum_start(sq_out, sl1, sl2, 1)
        sum_second(sl1, sl2, 1)

        def drain_rs(s, carry):
            rs_drain(s)
            return carry

        for s in range(3):
            rs_drain(s)
        lax.fori_loop(3, PIECES, drain_rs, 0)
        sum_end(sq_out, sl1, sl2, 1)
        gn_out[4:5, 0:128] = jnp.sum(sq_out[...], axis=0, keepdims=True)
        pltpu.make_async_copy(gbuf, g_out, loc.at[10]).wait()
    else:
        for j in range(3):
            g_copy = pltpu.make_async_copy(GA if j == 0 else W.at[j], g_out.at[j], loc.at[3 + j])
            g_copy.start()
            g_copy.wait()
    small_copy = pltpu.make_async_copy(gn_out, small_out, loc.at[11])
    small_copy.start()
    small_copy.wait()
    out_wait(lo_out, 0)
    out_wait(ig_out, 1)

    @pl.when(core == own)
    def _():
        for i in range(3):
            in_remote(i).wait_send()


def rope_tables(length):
    places = np.arange(length, dtype=np.float32)
    rates = (ROPE_BASE ** (-(np.arange(HD // 2, dtype=np.float32) * 2.0 / HD))).astype(np.float32)
    angles = places[:, None] * rates[None, :]
    cos = np.tile(np.cos(angles), (1, 4)).astype(np.float32)
    sin = np.tile(np.sin(angles), (1, 4)).astype(np.float32)
    first = (np.arange(128) % HD < HD // 2)[None, :]
    return np.stack([cos, np.where(first, -sin, sin)]).astype(np.float32)


def adam_update(refs, outs, gradient, clip_factor, step_rate, decay_rate):
    master, first_old, second_old = (ref[...] for ref in refs)
    clipped = gradient * clip_factor
    first_new = BETA_FIRST * first_old + (1.0 - BETA_FIRST) * clipped
    second_new = BETA_SECOND * second_old + (1.0 - BETA_SECOND) * clipped * clipped
    fix_first = 1.0 - BETA_FIRST**STEP
    fix_second = 1.0 - BETA_SECOND**STEP
    normalized = first_new / fix_first / (jnp.sqrt(second_new / fix_second) + ADAM_EPSILON)
    master_new = master - step_rate * (normalized + decay_rate * master)
    for out, v in zip(outs, (master_new, first_new, second_new, master_new.astype(BF16))):
        out[...] = v


def update_kernel(R, shapes, g_in, small_in, lo_in, ig_in, *refs):
    param_ins, refs = refs[:15], refs[15:]
    lo_out, ig_out, norm_out = refs[:3]
    param_outs, refs = refs[3:23], refs[23:]
    g, small, params, outs, in_sems, out_sems = refs[0], refs[1], refs[2:17], refs[17:37], refs[37], refs[38]
    passing = [(lo_in, refs[39].at[0], lo_out), (ig_in, refs[39].at[1], ig_out)]
    copies = [pltpu.make_async_copy(src, via, in_sems.at[17 + i]) for i, (src, via, _) in enumerate(passing)]
    ins = [pltpu.make_async_copy(g_in, g, in_sems.at[15]), pltpu.make_async_copy(small_in, small, in_sems.at[16])]
    ins += [pltpu.make_async_copy(src, dst, in_sems.at[i]) for i, (src, dst) in enumerate(zip(param_ins, params))]
    for copy in ins + copies:
        copy.start()
    for copy in ins + copies:
        copy.wait()
    copies = [pltpu.make_async_copy(via, dst, out_sems.at[20 + i]) for i, (_, via, dst) in enumerate(passing)]
    for copy in copies:
        copy.start()
    gn_all = small[0:4, :]
    squares = jnp.sum(small[4:5, 0:128], keepdims=True) + jnp.sum(gn_all * gn_all, keepdims=True)
    grad_norm = jnp.sqrt(squares)
    norm_out[...] = grad_norm
    clip_factor = jnp.minimum(1.0, CLIP_LIMIT / (grad_norm + 1e-06))

    def transposed(v):
        return jnp.concatenate([v, jnp.zeros((128 - R, v.shape[1]), F32)], axis=0).T[:, :R]

    a = g[0]
    g_proj = [jnp.concatenate([a[:, 128 * j : 128 * j + 128], a[:, 384 + 64 * j : 448 + 64 * j]], axis=1) for j in range(3)]
    g_out = transposed(jnp.concatenate([a[:, 640:], a[:, 576:640]], axis=1))
    D = gn_all.shape[1]
    first_row = lax.axis_index("dp") * R
    r_i = lax.broadcasted_iota(jnp.int32, (D, 128), 0)
    c_i = lax.broadcasted_iota(jnp.int32, (D, 128), 1)
    sel = jnp.where((r_i == c_i + first_row) & (c_i < R), 1.0, 0.0).astype(BF16)
    g_norm = sum(dot(part.astype(BF16), sel) for part in three_parts(small[...]))[:4, :R]

    def update(i, gradient, rate, decay, index=None):
        ins, results = params[3 * i : 3 * i + 3], outs[4 * i : 4 * i + 4]
        if index is not None:
            ins, results = [r.at[index] for r in ins], [r.at[index] for r in results]
        adam_update(ins, results, gradient, clip_factor, rate, decay)
        if index is None or index == 2:
            for n in range(4 * i, 4 * i + 4):
                copies.append(pltpu.make_async_copy(outs[n], param_outs[n], out_sems.at[n]))
                copies[-1].start()

    update(2, g[1], RATE_MATRIX, WEIGHT_DECAY)
    update(3, g[2], RATE_MATRIX, WEIGHT_DECAY)
    for j in range(3):
        update(0, g_proj[j], RATE_MATRIX, WEIGHT_DECAY, j)
    update(1, g_out, RATE_MATRIX, WEIGHT_DECAY)
    update(4, g_norm, RATE_NORM, 0.0)
    for copy in copies:
        copy.wait()


def per_device(
    inputs,
    cotangent,
    lengths,
    proj_master,
    proj_first,
    proj_second,
    out_master,
    out_first,
    out_second,
    up_master,
    up_first,
    up_second,
    down_master,
    down_first,
    down_second,
    norm_master,
    norm_first,
    norm_second,
):
    _, T, D = inputs.shape
    R = proj_master.shape[1]
    n_dp = lax.axis_size("dp")
    inner = n_dp == 8
    d = lax.axis_index("dp")
    z = lax.axis_index("head")
    core = d % 2
    if inner:
        norm_in = norm_master
        extra = (proj_master, out_master, up_master, down_master.T)
    else:
        out_t = out_master.T
        attn = jnp.concatenate(
            [proj_master[0, :, :128], proj_master[1, :, :128], proj_master[2, :, :128]]
            + [proj_master[0, :, 128:], proj_master[1, :, 128:], proj_master[2, :, 128:]]
            + [out_t[:, 128:], out_t[:, :128]],
            axis=1,
        )
        pack = jnp.stack([attn, up_master, down_master.T]).astype(BF16)
        norm_in = jnp.pad(lax.all_gather(norm_master, "dp", axis=1, tiled=True), ((0, 4), (0, 0)))
        norm_in = norm_in.astype(BF16).astype(F32)
        full = lax.all_gather(pack, "dp", axis=1, tiled=True)
        every = lax.all_gather(full, "head", axis=0)
        pair = lax.dynamic_slice_in_dim(every, 2 * core, 2, 0)
        w_in = jnp.concatenate([pair[0], pair[1]], axis=2)
        extra = (w_in,)

    hbm = pl.BlockSpec(memory_space=pltpu.HBM)
    dma = pltpu.SemaphoreType.DMA
    quarter = T // 4
    g_shape = (3, R, 768) if inner else (3, D, 1536)
    out_shape = (
        jax.ShapeDtypeStruct((2, quarter, D), BF16),
        jax.ShapeDtypeStruct((2, quarter, D), BF16),
        jax.ShapeDtypeStruct(g_shape, F32 if inner else BF16),
        jax.ShapeDtypeStruct((8, D), F32),
    )
    HALF = T // 2
    NB = T // 256
    bf = lambda *s: pltpu.VMEM(s, BF16)
    ff = lambda *s: pltpu.VMEM(s, F32)
    RC = 2 * R
    pieces = PIECES if inner else 1
    lx_rows = RC if inner else 16
    zl_rows = R if inner else 16
    RL = R if inner else 8
    scratch = [
        bf(3, D, 1536), bf(D, 1536), bf(T, D), bf(T, D), bf(D, T), bf(T, D), bf(D, T), bf(T, D), bf(D, T), ff(T, D),
        bf(6, T, 128), bf(6, T, 128), bf(6, T, 128), bf(6, T, 128), bf(3, 128, T),
        bf(3, T, 128), bf(3, T, 128), bf(2, D, 256), bf(T, 2 * SUB), bf(T, 1536), ff(T, D), bf(T, D), ff(128, T), ff(T, D),
        bf(HALF, D), bf(HALF, D), bf(HALF, D), bf(2, HALF, D),
        ff(8, 128), ff(8, 128), bf(3, zl_rows, 768), ff(8, D), ff(8, 8, 128), ff(8, 8, D), ff(4, 8, D), ff(8, 8, 128), ff(4, 8, 128),
        bf(pieces, 2, 2, lx_rows, SUB), bf(pieces, 2, lx_rows, SUB), bf(pieces, 4, zl_rows, SUB),
        dma((3,)), dma((3,)), dma((3,)), dma((3,)), dma((2,)), dma((2,)), dma((NB,)), dma((NB,)),
        dma((1,)), dma((1,)), dma((NB,)), dma((NB,)), dma((2, 2)), dma((2, 2)), dma((4,)), dma((4,)), dma((2, 11)), dma((2, 11)),
        dma((pieces, 4)), dma((pieces, 4)), dma((pieces, 2, 3)), dma((pieces, 2, 3)),
        dma((pieces, 2, 2)), dma((pieces, 2, 2)), dma((pieces, 2)), dma((pieces, 2)), dma((pieces, 4)), dma((pieces, 4)),
        dma((12,)),
        ff(2, T, 128), ff(*norm_in.shape), ff(3, RL, 192), ff(192, RL), ff(RL, 768), ff(RL, 768), ff(8, D), ff(8, 128), ff(3, RL, 768), ff(RL, SUB),
    ]
    layer_out, input_grad, grads, small = pl.pallas_call(
        functools.partial(layer_kernel, inner, T, D, R),
        out_shape=out_shape,
        in_specs=[hbm, hbm, pl.BlockSpec(memory_space=pltpu.SMEM)] + [hbm] * (2 + len(extra)),
        out_specs=(hbm,) * 4,
        scratch_shapes=scratch,
        compiler_params=pltpu.CompilerParams(
            collective_id=0, has_side_effects=True, vmem_limit_bytes=63 * 2**20
        ),
        name="layer",
    )(inputs, cotangent, lengths, jnp.asarray(rope_tables(T)), norm_in, *extra)

    if not inner:
        spread = jnp.stack([grads[:, :, :768], grads[:, :, 768:]]).astype(F32)
        empty = jnp.zeros((4,) + spread.shape[1:], F32)
        spread = lax.dynamic_update_slice_in_dim(empty, spread, 2 * core, 0)
        mine = lax.psum_scatter(spread, "head", scatter_dimension=0, tiled=False)
        grads = lax.psum_scatter(mine, "dp", scatter_dimension=1, tiled=True)
        squares = lax.psum(jnp.sum(grads * grads), ("dp", "head"))
        small = lax.psum(small, ("dp", "head")).at[4, 0].set(squares)
    params = (
        (proj_master, proj_first, proj_second),
        (out_master, out_first, out_second),
        (up_master, up_first, up_second),
        (down_master.T, down_first.T, down_second.T),
        (norm_master, norm_first, norm_second),
    )
    shapes = []
    for group in params:
        shapes += [(v.shape, F32) for v in group] + [(group[0].shape, BF16)]
    out_shapes = [((2, quarter, D), BF16)] * 2 + [((1, 1), F32)] + shapes
    flat = [v for group in params for v in group]
    outs = pl.pallas_call(
        functools.partial(update_kernel, R, shapes),
        out_shape=tuple(jax.ShapeDtypeStruct(*v) for v in out_shapes),
        in_specs=[hbm] * 19,
        out_specs=tuple([hbm] * 2 + [pl.BlockSpec(memory_space=pltpu.VMEM)] + [hbm] * 20),
        scratch_shapes=[ff(*grads.shape), ff(8, D)]
        + [ff(*v.shape) for v in flat]
        + [pltpu.VMEM(*v) for v in shapes]
        + [dma((19,)), dma((22,)), bf(2, 2, quarter, D)],
        compiler_params=pltpu.CompilerParams(vmem_limit_bytes=63 * 2**20),
        name="update",
    )(grads, small, layer_out, input_grad, *flat)
    down = tuple(v.T for v in outs[15:19])
    return tuple(outs[:2]) + (outs[2].reshape(()),) + tuple(outs[3:15]) + down + tuple(outs[19:])


def solution(mesh):
    proj, wide, tall, norms = P(None, "dp", "head"), P("dp", "head"), P("head", "dp"), P(None, "dp")
    tokens = P("dp", None, None)
    placed = (tokens, tokens, P("dp")) + (proj,) * 3 + (tall,) * 3 + (wide,) * 3 + (tall,) * 3 + (norms,) * 3
    quarters = P("dp", "head", None)
    return jax.shard_map(
        per_device,
        mesh=mesh,
        in_specs=placed,
        out_specs=(quarters, quarters, P()) + (proj,) * 4 + (tall,) * 4 + (wide,) * 4 + (tall,) * 4 + (norms,) * 4,
        check_vma=False,
    )
```

time: 255 us -> 187 us (0.73)
  Pallas kernels: 228 us -> 186 us
  other arithmetic: 13.4 us -> 0 us
  local copies, waits for them, and re-layouts: 8.98 us -> 0 us
  between operations: 4.1 us -> 0.87 us
    pallas_call x1, Pallas kernels: 228 us -> 179 us  [per_device(): pl.pallas_call(functools.partial(layer_kernel, inner, T, D, R), out_shape...]
    pallas_call x0 -> x1, Pallas kernels: none -> 6.41 us  [per_device(): pl.pallas_call(functools.partial(update_kernel, R, shapes), out_shape=tup...]
    convert_element_type x6 -> x0, other arithmetic: 6.37 us -> none  [the longest x5 6.36 us: adam_update(): return (master_new, first_new, second_new, master_new.astype(BF16))]
    unnamed x37 -> x0, local copies, waits for them, and re-layouts: 5.92 us -> none
    another operation x7 -> x0, other arithmetic: 3.79 us -> none  [the longest x3 2.78 us: per_device(): pack = jnp.stack([attn, up_master, down_master.T]).astype(BF16)]
where the time goes in v2:
time: 187 us; the launch traced here: 186 us
  Pallas kernels  186 us (99%)
    pallas_call x1, Pallas kernels, per_device(): pl.pallas_call(functools.partial(layer_kernel, inner, T, D, R), out_shape...  179 us
    pallas_call x1, Pallas kernels, per_device(): pl.pallas_call(functools.partial(update_kernel, R, shapes), out_shape=tup...  6.41 us

profile of v2, /device:TPU:0, one launch (start us, length us, event | category | flops | bytes accessed | tf_op | source)
XLA Modules:
  0.0 186.4 jit_solution(8831662633100488792)
XLA Ops:
  0.7 179.1 %layer.1 = (bf16[2,256,768]{2,1,0:T(8,128)(2,1)}, bf16[2,256,768]{2,1,0:T(8,128)(2,1)}, f32[3,96,768]{2,1,0:T(8,128)}, f32[8,768]{1,0:T(8,128)}) custom-call(bf16[2,1024,768]{2,1,0:T(8,128)(2,1)} %refs_0_.2, bf16[2,1024,768]{2,1,0:T(8,128)(2,1)} %refs_1_.2, s32[2]{0:T(128)} %refs_2_.2, f32[2,1024,128]{2,1,0:T(8,128)} %constant.2.clone.refs_3_, ...), custom_call_target="tpu_custom_call" | custom-call | tf_op jit(solution)/shard_map/layer/pallas_call | solution.py:1082
  179.8 6.4 %update.1 = (bf16[2,256,768]{2,1,0:T(8,128)(2,1)}, bf16[2,256,768]{2,1,0:T(8,128)(2,1)}, f32[1,1]{1,0:T(1,128)}, f32[3,96,192]{2,1,0:T(8,128)}, f32[3,96,192]{2,...) custom-call(f32[3,96,768]{2,1,0:T(8,128)} %get-tuple-element.50.g_in, ...), custom_call_target="tpu_custom_call" | custom-call | tf_op jit(solution)/shard_map/update/pallas_call | solution.py:1114
